TPU v7x, 512 devices: a whole 4x8x8 slice. The times are simulated.
512 devices in a mesh: gx: 4 (over x), gy: 4 (over y_lo), gz: 32 (over y_hi, z, core).
Axes of the slice: x: 4, y: 8 (y_hi: 2, y_lo: 4; y = y_hi * 4 + y_lo), z: 8, core: 2. Of those that a mesh axis runs over, the one named last changes fastest.
Arguments:
- features: bfloat16 [4, 4, 32, 256, 128], P('gx', 'gy', 'gz'), may hold values from -6 to 6
- positions: float32 [4, 4, 32, 3, 256], P('gx', 'gy', 'gz'), may hold values from 0 to 1
- counts: int32 [4, 4, 32], P('gx', 'gy', 'gz'), may hold values from 128 to 256, as said below
- pair_tiles: int32 [4, 4, 32, 14, 2, 2], P('gx', 'gy', 'gz'), may hold values from 0 to 7, as said below
- input_weight: bfloat16 [128, 128], replicated, may hold values from -0.5 to 0.5
- radial_weight: bfloat16 [128, 128], replicated, may hold values from -1.5 to 1.5
- radial_bias: float32 [128], replicated, may hold values from -3 to 3
- filter_weight: bfloat16 [128, 128], replicated, may hold values from -0.5 to 0.5
- filter_bias: float32 [128], replicated, may hold values from -3 to 3
- output_weight: bfloat16 [128, 128], replicated, may hold values from -0.1875 to 0.1875
- output_bias: float32 [128], replicated, may hold values from -3 to 3
- final_weight: bfloat16 [128, 128], replicated, may hold values from -0.5 to 0.5
- final_bias: float32 [128], replicated, may hold values from -3 to 3
- cotangent: bfloat16 [4, 4, 32, 256, 128], P('gx', 'gy', 'gz'), may hold values from -1.5 to 1.5
Outputs:
- new_features: bfloat16 [4, 4, 32, 256, 128], P('gx', 'gy', 'gz')
- grad_features: float32 [4, 4, 32, 256, 128], P('gx', 'gy', 'gz')
- forces: float32 [4, 4, 32, 3, 256], P('gx', 'gy', 'gz')
Inputs may be any that keep to these rules, and one draw needn't show every extreme that they name: Block p holds counts[p] atoms in its first slots; the other slots are empty. Some block is full. `pair_tiles`: for each block and each of the 14 offsets, the 2 entries are distinct pairs (a, b) of tile numbers below 8; for offset 0 every pair has a <= b.
All inputs are finite; a program needn't handle non-finite values.
Results may differ from a plain program's by a relative error of at most 0.0085.
Values sent between devices are 32-bit elements; how exact they have to be, the bound alone decides.
No kernel may reach another device: no remote copies, remote signals or barrier semaphores. Data moves between devices by JAX's collectives and lax.ppermute only.
A program may use at most 192 MiB of HBM per device.

v0:
```python
import math

import jax
import jax.numpy as jnp
import numpy as np
from jax import lax
from jax.experimental import pallas as pl
from jax.experimental.pallas import tpu as pltpu
from jax.sharding import PartitionSpec as P

TILE = 32
SOFTEN = 0.05
GAMMA = 40.0
LOG_TWO = math.log(2.0)
KAPPA = math.sqrt(GAMMA / LOG_TWO)
UNITS = 56
VMEM = 56 * 1024 * 1024


def half_shell():
    offsets = [(0, 0, 0), (1, 0, 0)]
    for step_x in (-1, 0, 1):
        offsets.append((step_x, 1, 0))
    for step_x in (-1, 0, 1):
        for step_y in (-1, 0, 1):
            offsets.append((step_x, step_y, 1))
    return offsets


SHELL = half_shell()
AROUND = [
    (sx, sy, sz)
    for sy in (0, 1, -1)
    for sx in (-1, 0, 1)
    for sz in (-1, 0, 1)
    if (sx, sy, sz) != (0, 0, 0)
]
SLOTS = [(0, 0, 0), (0, 0, 0)] + AROUND


def shell_place(offset):
    if offset in SHELL:
        return SHELL.index(offset), True
    return SHELL.index(tuple(-step for step in offset)), False


def pair_rows():
    rows = [(SLOTS[0], SLOTS[0], 0, True), (SLOTS[0], SLOTS[0], 0, False)]
    rows += [(SLOTS[0], o, *shell_place(o)) for o in AROUND]
    for side in (1, -1):
        for sx in (-1, 0, 1):
            for sz in (-1, 0, 1):
                rows.append(((0, -side, 0), (sx, side, sz), *shell_place((sx, side, sz))))
    picked = np.zeros((len(rows), 28 * 14), np.float32)
    forward = np.zeros((len(rows), 1), bool)
    for i, (reader, offset, index_k, ahead) in enumerate(rows):
        holder = reader if ahead else tuple(a + b for a, b in zip(reader, offset))
        picked[i, SLOTS.index(holder) * 14 + index_k] = 1.0
        forward[i, 0] = ahead
    return picked, forward


def whole(array):
    return pl.BlockSpec(array.shape, lambda s, *_: (0,) * array.ndim)


def exact_dot(a, b):
    return jnp.dot(a, b, precision=lax.Precision.HIGHEST)


BODY = 16
ROWS = BODY * TILE
SLABS = UNITS * TILE
BODIES = SLABS // BODY
STEP = 8
STEPS = BODIES // STEP


def last_block(step, count):
    return jnp.minimum(step, jnp.maximum((count[0] + STEP - 1) // STEP - 1, 0))


def bodies_of(step, count):
    return jnp.clip(count[0] - step * STEP, 0, STEP)


def filter_kernel(count, order, table, centres, first_w, second_w, first_b, second_b, out, out_d):
    step = pl.program_id(0)

    def one(index, carry):
        spread = [[], [], [], []]
        for j in range(BODY):
            slab = order[(step * STEP + index) * BODY + j]
            lanes = pl.ds(pl.multiple_of(slab // 128 * 128, 128), 128)
            lane = jnp.full((TILE, 128), slab % 128, jnp.int32)
            for q in range(4):
                values = table[q * TILE : (q + 1) * TILE, lanes]
                spread[q].append(jnp.take_along_axis(values, lane, axis=1, mode="promise_in_bounds"))
        x = jnp.concatenate(spread[0], axis=0) - centres[...]
        e = jnp.exp2(-(x * x))
        both = jnp.concatenate([e.astype(jnp.bfloat16), (x * e).astype(jnp.bfloat16)], axis=1)
        first = jnp.dot(both, first_w[...], preferred_element_type=jnp.float32)
        z = 1.0 + jnp.exp(first[:, 0:128] + first_b[...])
        act = jnp.log(z) - LOG_TWO
        deriv = first[:, 128:256]
        deriv = deriv - deriv * pl.reciprocal(z, approx=True)
        both2 = jnp.concatenate([act.astype(jnp.bfloat16), deriv.astype(jnp.bfloat16)], axis=1)
        second = jnp.dot(both2, second_w[...], preferred_element_type=jnp.float32)
        base = second[:, 0:128] + second_b[...]
        at_row = pl.ds(pl.multiple_of(index * ROWS, ROWS), ROWS)
        out[at_row, :] = (base * jnp.concatenate(spread[1], axis=0)).astype(jnp.bfloat16)
        out_d[at_row, :] = (
            second[:, 128:256] * jnp.concatenate(spread[2], axis=0)
            + base * jnp.concatenate(spread[3], axis=0)
        ).astype(jnp.bfloat16)
        return carry

    lax.fori_loop(0, bodies_of(step, count), one, 0)


def filters(count, order, table, first_w, second_w, first_b, second_b):
    centres = np.array(KAPPA * np.arange(128) / 128.0, np.float32)[None]
    arrays = [table, jnp.asarray(centres), first_w, second_w, first_b, second_b]
    wide = pl.BlockSpec((STEP * ROWS, 128), lambda s, n, *_: (last_block(s, n), 0))
    return pl.pallas_call(
        filter_kernel,
        grid_spec=pltpu.PrefetchScalarGridSpec(
            num_scalar_prefetch=2,
            grid=(STEPS,),
            in_specs=[whole(a) for a in arrays],
            out_specs=[wide, wide],
        ),
        out_shape=[jax.ShapeDtypeStruct((SLABS * TILE, 128), jnp.bfloat16)] * 2,
        compiler_params=pltpu.CompilerParams(vmem_limit_bytes=VMEM),
        name="pair_filters",
    )(count, order, *arrays)


def gather_kernel(starts, table, up, down):
    def one(index, carry):
        a = pl.multiple_of(starts[index], TILE)
        b = pl.multiple_of(starts[18 + index], TILE)
        o = pl.multiple_of(index * TILE, TILE)
        up[pl.ds(o, TILE), :] = table[pl.ds(a, TILE), :]
        down[pl.ds(o, TILE), :] = table[pl.ds(b, TILE), :]
        return carry

    lax.fori_loop(0, 18, one, 0)


def gather_tiles(starts, table):
    shape = (18 * TILE, 128)
    whole = pl.BlockSpec(shape, lambda s, *_: (0, 0))
    return pl.pallas_call(
        gather_kernel,
        grid_spec=pltpu.PrefetchScalarGridSpec(
            num_scalar_prefetch=1,
            grid=(1,),
            in_specs=[pl.BlockSpec(table.shape, lambda s, *_: (0, 0))],
            out_specs=[whole, whole],
        ),
        out_shape=[jax.ShapeDtypeStruct(shape, jnp.float32)] * 2,
        compiler_params=pltpu.CompilerParams(vmem_limit_bytes=VMEM),
        name="tiles_to_send",
    )(starts, table)


def softplus(values):
    return jnp.maximum(values, 0.0) + jnp.log(1.0 + jnp.exp(-jnp.abs(values)))


def nt_dot(a, b):
    return lax.dot_general(a, b, (((1,), (1,)), ((), ())), preferred_element_type=jnp.float32)


CHAINS = 4


def message_kernel(
    count, order, tiles, starts, filt, near, feats, cot, out_w, out_b, fin_w, fin_b, new, grad, *totals
):
    step = pl.program_id(0)

    @pl.when(step == 0)
    def _():
        for total in totals:
            total[...] = jnp.zeros_like(total)

    def one(index, carry):
        for j in range(BODY):
            slab = order[(step * STEP + index) * BODY + j]
            unit = slab // TILE
            h = near[pl.ds(starts[unit] + slab % TILE, 1), :]
            rows = pl.ds(pl.multiple_of(index * ROWS + j * TILE, TILE), TILE)
            own = pl.ds(pl.multiple_of(tiles[unit] * TILE, TILE), TILE)
            total = totals[j % CHAINS]
            total[own, :] = total[own, :] + filt[rows, :].astype(jnp.float32) * h
        return carry

    lax.fori_loop(0, bodies_of(step, count), one, 0)

    @pl.when(step == pl.num_programs(0) - 1)
    def _():
        cast = sum(total[...] for total in totals).astype(jnp.bfloat16)
        pre = jnp.dot(cast, out_w[...], preferred_element_type=jnp.float32) + out_b[...]
        act = (softplus(pre) - LOG_TWO).astype(jnp.bfloat16)
        update = jnp.dot(act, fin_w[...], preferred_element_type=jnp.float32) + fin_b[...]
        new[...] = (feats[...].astype(jnp.float32) + update).astype(jnp.bfloat16)
        d_out = nt_dot(cot[...], fin_w[...])
        d_pre = (d_out * jax.nn.sigmoid(pre)).astype(jnp.bfloat16)
        grad[...] = nt_dot(d_pre, out_w[...])


def back_kernel(
    count, order, tiles, starts, filt, filt_d, near, g_near, own_h, own_g, r_near, r_own, cot, in_w,
    grad, force, *totals
):
    step = pl.program_id(0)
    pushes = totals[CHAINS:]
    totals = totals[:CHAINS]

    @pl.when(step == 0)
    def _():
        for total in (*totals, *pushes):
            total[...] = jnp.zeros_like(total)

    def one(index, carry):
        slopes = []
        places = []
        for j in range(BODY):
            slab = order[(step * STEP + index) * BODY + j]
            unit = slab // TILE
            row = pl.ds(starts[unit] + slab % TILE, 1)
            h = near[row, :]
            g = g_near[row, :]
            rows = pl.ds(pl.multiple_of(index * ROWS + j * TILE, TILE), TILE)
            own = pl.ds(pl.multiple_of(tiles[unit] * TILE, TILE), TILE)
            total = totals[j % CHAINS]
            total[own, :] = total[own, :] + filt[rows, :].astype(jnp.float32) * g
            mixed = filt_d[rows, :].astype(jnp.float32) * (own_g[own, :] * h + own_h[own, :] * g)
            slopes.append(mixed.astype(jnp.bfloat16))
            places.append((own, slab))
        sums = jnp.dot(
            jnp.concatenate(slopes, axis=0),
            jnp.ones((128, 128), jnp.bfloat16),
            preferred_element_type=jnp.float32,
        )
        for j, (own, slab) in enumerate(places):
            push = pushes[j % CHAINS]
            away = r_near[pl.ds(slab, 1), :] - r_own[own, :]
            push[own, :] = push[own, :] + sums[j * TILE : (j + 1) * TILE, :] * away
        return carry

    lax.fori_loop(0, bodies_of(step, count), one, 0)

    @pl.when(step == pl.num_programs(0) - 1)
    def _():
        cast = sum(total[...] for total in totals).astype(jnp.bfloat16)
        grad[...] = cot[...].astype(jnp.float32) + nt_dot(cast, in_w[...])
        force[...] = sum(push[...] for push in pushes).T[0:8, :]


def pair_call(body, scalars, streams, arrays, outs, scratch, name):
    stream = pl.BlockSpec((STEP * ROWS, 128), lambda s, n, *_: (last_block(s, n), 0))
    return pl.pallas_call(
        body,
        grid_spec=pltpu.PrefetchScalarGridSpec(
            num_scalar_prefetch=4,
            grid=(STEPS,),
            in_specs=[stream] * len(streams) + [whole(a) for a in arrays],
            out_specs=[whole(o) for o in outs],
            scratch_shapes=[pltpu.VMEM((256, 128), jnp.float32)] * scratch,
        ),
        out_shape=outs,
        compiler_params=pltpu.CompilerParams(vmem_limit_bytes=VMEM),
        name=name,
    )(*scalars, *streams, *arrays)


def moved(x, axis, by):
    size = lax.axis_size(axis)
    return lax.ppermute(x, axis, [((i + by) % size, i) for i in range(size)])


def planes(own):
    return jnp.concatenate([moved(own, "gz", -1), own, moved(own, "gz", 1)], axis=0)


def columns(three):
    return jnp.concatenate([moved(three, "gx", -1), three, moved(three, "gx", 1)], axis=0)


def rows_around(nine, wanted):
    to_lower, to_upper = gather_tiles(wanted, nine)
    return jnp.concatenate([nine, moved(to_lower, "gy", 1), moved(to_upper, "gy", -1)], axis=0)


def block_diagonal(weight):
    zero = jnp.zeros_like(weight)
    return jnp.concatenate(
        [jnp.concatenate([weight, zero], axis=1), jnp.concatenate([zero, weight], axis=1)], axis=0
    )


def on_device(
    features,
    positions,
    counts,
    pair_tiles,
    input_weight,
    radial_weight,
    radial_bias,
    filter_weight,
    filter_bias,
    output_weight,
    output_bias,
    final_weight,
    final_bias,
    cotangent,
):
    own_features = features.reshape(256, 128)
    own_pos = positions.reshape(3, 256)
    hidden = jnp.dot(own_features, input_weight, preferred_element_type=jnp.float32)
    numbers = jnp.concatenate([counts.reshape(1), pair_tiles.reshape(56)]).astype(jnp.float32)
    meta = jnp.concatenate(
        [own_pos.reshape(6, 128), jnp.pad(numbers, (0, 71))[None], jnp.zeros((1, 128), jnp.float32)],
        axis=0,
    )
    three = planes(jnp.concatenate([hidden, meta], axis=0)[None])
    meta_three = three[:, 256:].reshape(1, 24 * 128)
    hidden_three = three[:, :256].reshape(768, 128)

    across = lax.axis_size("gy")
    along = lax.axis_size("gx")
    everyone = lax.all_to_all(
        jnp.broadcast_to(meta_three.reshape(1, 24, 128), (along * across, 24, 128)),
        ("gx", "gy"),
        0,
        0,
    ).reshape(along * across, 24 * 128)
    everyone = everyone.reshape(along * across * 3, 8 * 128)
    side = np.array(SLOTS)
    holders = (lax.axis_index("gx") + side[:, 0]) % along * across
    holders = (holders + (lax.axis_index("gy") + side[:, 1]) % across) * 3 + side[:, 2] + 1
    picker = (holders[:, None] == jnp.arange(along * across * 3)[None, :]).astype(jnp.float32)
    slots = exact_dot(picker, everyone)

    picked, forward = pair_rows()
    lists = exact_dot(picked, slots[:, 769:825].reshape(28 * 14, 4))
    lists = jnp.round(lists).astype(jnp.int32)
    mine = jnp.where(forward, lists[:, 0:2], lists[:, 2:4])
    theirs = jnp.where(forward, lists[:, 2:4], lists[:, 0:2])
    own_tiles, other_tiles = mine[:28], theirs[:28]
    column = ((side[:, 0] + 1) * 3 + side[:, 2] + 1)[:, None]
    entry = np.arange(2)[None]
    starts = jnp.where(
        (side[:, 1] == 0)[:, None],
        column * 256 + other_tiles * TILE,
        2304 + 576 * (side[:, 1:2] < 0) + (column * 2 + entry) * TILE,
    )
    wanted = (np.tile(np.arange(9), 2)[:, None] * 256 + theirs[28:] * TILE).reshape(36)

    pick_other = (other_tiles[:, :, None] == jnp.arange(8)).astype(jnp.float32)
    slot_pos = slots[:, : 6 * 128].reshape(28, 1, 3, 8, TILE)
    shift = np.repeat(np.array(SLOTS, np.float32), 2, axis=0)
    other_at = jnp.sum(pick_other[:, :, None, :, None] * slot_pos, axis=3).reshape(UNITS, 3, TILE)
    other_at = other_at + shift[:, :, None]
    same = ((own_tiles == other_tiles) & (np.arange(28) < 2)[:, None]).astype(jnp.float32)
    per_unit = jnp.stack(
        [
            own_tiles.astype(jnp.float32),
            slots[0:1, 768:769] - own_tiles * TILE,
            slots[:, 768:769] - other_tiles * TILE,
            same,
        ]
    ).reshape(4, UNITS)
    slab = np.arange(SLABS)
    per_slab = exact_dot(per_unit, (slab[None] // TILE == np.arange(UNITS)[:, None]).astype(np.float32))
    own_side = own_pos.reshape(3, 8, TILE).transpose(0, 2, 1).reshape(96, 8)
    own_at = exact_dot(
        own_side, (per_slab[0:1] == np.arange(8, dtype=np.float32)[:, None]).astype(jnp.float32)
    ).reshape(3, TILE, SLABS)
    other_row = other_at.transpose(1, 0, 2).reshape(3, 1, SLABS)
    sep = other_row - own_at
    dist = jnp.sqrt(sep[0] * sep[0] + sep[1] * sep[1] + sep[2] * sep[2] + SOFTEN * SOFTEN)
    w = jnp.asarray(slab % TILE, jnp.float32)[None]
    u = jnp.asarray(np.arange(TILE), jnp.float32)[:, None]
    reverse = jnp.asarray(slab // TILE >= 2)[None]
    drop = (per_slab[3:4] > 0.5) & jnp.where(reverse, w >= u, u >= w)
    usable = (u < per_slab[1:2]) & (w < per_slab[2:3]) & (dist < 1.0) & ~drop
    angle = math.pi * dist
    cut = jnp.where(usable, 0.5 * (jnp.cos(angle) + 1.0), 0.0)
    gain = cut * (-2.0 * GAMMA / KAPPA) / dist
    slope = jnp.where(usable, -0.5 * math.pi * jnp.sin(angle), 0.0) / dist
    table = jnp.pad(
        jnp.concatenate([KAPPA * dist, cut, gain, slope], axis=0), ((0, 0), (0, 128))
    )
    live = jnp.max(usable.astype(jnp.float32), axis=0).reshape(SLABS // 128, 128)
    until = exact_dot(live, np.triu(np.ones((128, 128), np.float32)))
    before = exact_dot(np.tril(np.ones((14, 14), np.float32), -1), until[:, 127:128])
    rank = jnp.where(live > 0.5, until + before - 1.0, -1.0).reshape(1, SLABS)
    total = jnp.sum(live).astype(jnp.int32)
    hit = rank == jnp.asarray(slab, jnp.float32)[:, None]
    order = jnp.sum(jnp.where(hit, jnp.asarray(slab)[None], 0), axis=1)
    order = jnp.where(slab < total, order, SLABS).astype(jnp.int32)
    count = ((total + BODY - 1) // BODY).reshape(1)

    filt, filt_d = filters(
        count,
        order,
        table,
        block_diagonal(radial_weight),
        block_diagonal(filter_weight),
        radial_bias[None],
        filter_bias[None],
    )
    near = rows_around(columns(hidden_three), wanted)
    cot = cotangent.reshape(256, 128)
    scalars = (
        count,
        order,
        jnp.pad(own_tiles.reshape(UNITS), (0, 8)),
        jnp.pad(starts.reshape(UNITS), (0, 8)).astype(jnp.int32),
    )
    new_features, d_msg = pair_call(
        message_kernel,
        scalars,
        [filt],
        [
            near,
            own_features,
            cot,
            output_weight,
            output_bias[None],
            final_weight,
            final_bias[None],
        ],
        [
            jax.ShapeDtypeStruct((256, 128), jnp.bfloat16),
            jax.ShapeDtypeStruct((256, 128), jnp.float32),
        ],
        CHAINS,
        "messages_and_update",
    )
    g_near = rows_around(columns(planes(d_msg)), wanted)
    r_near = jnp.pad(other_at.transpose(0, 2, 1).reshape(SLABS, 3), ((0, 8), (0, 125)))
    r_own = jnp.pad(own_pos.T, ((0, 0), (0, 125)))
    grad_features, force = pair_call(
        back_kernel,
        scalars,
        [filt, filt_d],
        [near, g_near, hidden, d_msg, r_near, r_own, cot, input_weight],
        [
            jax.ShapeDtypeStruct((256, 128), jnp.float32),
            jax.ShapeDtypeStruct((8, 256), jnp.float32),
        ],
        2 * CHAINS,
        "pair_gradients",
    )
    return (
        new_features.reshape(1, 1, 1, 256, 128),
        grad_features.reshape(1, 1, 1, 256, 128),
        force[:3].reshape(1, 1, 1, 3, 256),
    )


def solution(mesh):
    block = P("gx", "gy", "gz", None, None)
    return jax.shard_map(
        on_device,
        mesh=mesh,
        in_specs=(
            block,
            block,
            P("gx", "gy", "gz"),
            P("gx", "gy", "gz", None, None, None),
            *([P()] * 9),
            block,
        ),
        out_specs=(block, block, block),
        check_vma=False,
    )
```

profile of v0, /device:TPU:58, one launch (start us, length us, event | category | flops | bytes accessed | tf_op | source)
XLA Modules:
  0.0 191.9 jit_solution(18269186161831504781)
XLA Ops:
  4.2 12.8 %collective-permute-start.1 = (f32[1,264,128]{2,1,0:T(8,128)S(1)}, f32[1,264,128]{2,1,0:T(8,128)S(1)}, u32[]{:S(2)}, u32[]{:S(2)}) collective-permute-start(f32[1,264,128]{2,1,0:T(8,128)S(1)} %maximum_bitcast_fusion), channel_id=1, source_target_pairs={{1,0},{2,1},{3,2},{4,3},{5,4},{6,5},{7,6},{8,7},{9,8},{10,9},{11,1... | collective-permute-start | bytes 405512 | tf_op jit(solution)/shard_map/ppermute | solution.py:282
  17.0 1.9 %collective-permute-start = (f32[1,264,128]{2,1,0:T(8,128)S(1)}, f32[1,264,128]{2,1,0:T(8,128)S(1)}, u32[]{:S(2)}, u32[]{:S(2)}) collective-permute-start(f32[1,264,128]{2,1,0:T(8,128)S(1)} %maximum_bitcast_fusion), channel_id=1, source_target_pairs={{31,0},{0,1},{1,2},{2,3},{3,4},{4,5},{5,6},{6,7},{7,8},{8,9},{9,10... | collective-permute-start | bytes 405512 | tf_op jit(solution)/shard_map/ppermute | solution.py:282
  19.5 9.8 %collective-permute-done = f32[1,264,128]{2,1,0:T(8,128)S(1)} collective-permute-done((f32[1,264,128]{2,1,0:T(8,128)S(1)}, f32[1,264,128]{2,1,0:T(8,128)S(1)}, u32[]{:S(2)}, u32[]{:S(2)}) %collective-permute-start) | collective-permute-done | bytes 135200 | tf_op jit(solution)/shard_map/ppermute | solution.py:282
  30.1 7.9 %all-to-all-start = ((f32[16,24,128]{2,1,0:T(8,128)}), f32[16,24,128]{2,1,0:T(8,128)S(1)}, u32[]{:S(2)}, u32[]{:S(2)}) async-start(f32[16,24,128]{2,1,0:T(8,128)} %broadcast_in_dim.100), calls=%async_computation | async-start | bytes 393216 | tf_op jit(solution)/shard_map/all_to_all | solution.py:335
  37.9 1.5 fusion.18
  39.7 3.4 %collective-permute-start.2 = (f32[768,128]{1,0:T(8,128)S(1)}, f32[768,128]{1,0:T(8,128)S(1)}, u32[]{:S(2)}, u32[]{:S(2)}) collective-permute-start(f32[768,128]{1,0:T(8,128)S(1)} %bitcast.70), channel_id=1, source_target_pairs={{384,0},{0,128},{128,256},{256,384},{385,1},{1,129},{129,257},{257... | collective-permute-start | bytes 1179656 | tf_op jit(solution)/shard_map/ppermute | solution.py:282
  43.1 2.5 %collective-permute-start.3 = (f32[768,128]{1,0:T(8,128)S(1)}, f32[768,128]{1,0:T(8,128)S(1)}, u32[]{:S(2)}, u32[]{:S(2)}) collective-permute-start(f32[768,128]{1,0:T(8,128)S(1)} %bitcast.71), channel_id=1, source_target_pairs={{128,0},{256,128},{384,256},{0,384},{129,1},{257,129},{385,257},{1... | collective-permute-start | bytes 1179656 | tf_op jit(solution)/shard_map/ppermute | solution.py:282
  54.3 1.5 fusion
  58.7 1.1 select_maximum_fusion.table
  59.8 33.3 %pair_filters.1 = (bf16[57344,128]{1,0:T(8,128)(2,1)}, bf16[57344,128]{1,0:T(8,128)(2,1)}) custom-call(s32[1]{0:T(128)} %bitcast.14.count, s32[1792]{0:T(1024)} %fusion.26.order, f32[128,1920]{1,0:T(8,128)} %select_maximum_fusion.table, f32[1,128]{1,0:T(1,128)} %constant.143.clone.centres, bf16[256,256]{1,0:T(8,128)(2,1)} %get-tuple-element.62.first_w, ...), custom_call_target="tpu_custom_call" | custom-call | tf_op jit(solution)/shard_map/pair_filters/pallas_call | solution.py:125
  93.1 1.1 pad_maximum_fusion.table
  94.2 2.8 %tiles_to_send.2 = (f32[576,128]{1,0:T(8,128)}, f32[576,128]{1,0:T(8,128)}) custom-call(s32[36]{0:T(128)} %reshape.116.starts, f32[2304,128]{1,0:T(8,128)} %pad_maximum_fusion.table), custom_call_target="tpu_custom_call" | custom-call | tf_op jit(solution)/shard_map/tiles_to_send/pallas_call | solution.py:154
  97.1 1.9 collective-permute-start.4
  99.0 5.7 %collective-permute-start.5 = (f32[576,128]{1,0:T(8,128)}, f32[576,128]{1,0:T(8,128)S(1)}, u32[]{:S(2)}, u32[]{:S(2)}) collective-permute-start(f32[576,128]{1,0:T(8,128)} %get-tuple-element.15), channel_id=1, source_target_pairs={{96,0},{0,32},{32,64},{64,96},{97,1},{1,33},{33,65},{65,97},{98,2}... | collective-permute-start | bytes 884744 | tf_op jit(solution)/shard_map/ppermute | solution.py:282
  104.8 3.0 %collective-permute-done.4 = f32[576,128]{1,0:T(8,128)S(1)} collective-permute-done((f32[576,128]{1,0:T(8,128)}, f32[576,128]{1,0:T(8,128)S(1)}, u32[]{:S(2)}, u32[]{:S(2)}) %collective-permute-start.4) | collective-permute-done | bytes 294944 | tf_op jit(solution)/shard_map/ppermute | solution.py:282
  107.8 3.0 %collective-permute-done.5 = f32[576,128]{1,0:T(8,128)S(1)} collective-permute-done((f32[576,128]{1,0:T(8,128)}, f32[576,128]{1,0:T(8,128)S(1)}, u32[]{:S(2)}, u32[]{:S(2)}) %collective-permute-start.5) | collective-permute-done | bytes 294944 | tf_op jit(solution)/shard_map/ppermute | solution.py:282
  110.9 1.2 copy-done
  112.1 12.1 %messages_and_update.1 = (bf16[256,128]{1,0:T(8,128)(2,1)}, f32[256,128]{1,0:T(8,128)}) custom-call(s32[1]{0:T(128)} %bitcast.14.count, s32[1792]{0:T(1024)} %fusion.26.order, s32[64]{0:T(128)} %pad.28.tiles, s32[64]{0:T(128)} %pad.29.starts, bf16[57344,128]{1,0:T(8,128)(2,1)} %get-tuple-element.13.filt, f32[3456,128]{1,0:T(8,128)} %copy-done, ...), custom_call_target="tpu_custom_call" | custom-call | tf_op jit(solution)/shard_map/messages_and_update/pallas_call | solution.py:265
  124.2 2.0 %collective-permute-start.6 = (f32[256,128]{1,0:T(8,128)}, f32[256,128]{1,0:T(8,128)S(1)}, u32[]{:S(2)}, u32[]{:S(2)}) collective-permute-start(f32[256,128]{1,0:T(8,128)} %get-tuple-element.18.own_g), channel_id=1, source_target_pairs={{31,0},{0,1},{1,2},{2,3},{3,4},{4,5},{5,6},{6,7},{7,8},{8,9},{9,10... | collective-permute-start | bytes 393224 | tf_op jit(solution)/shard_map/ppermute | solution.py:282
  126.2 9.7 %collective-permute-start.7 = (f32[256,128]{1,0:T(8,128)}, f32[256,128]{1,0:T(8,128)S(1)}, u32[]{:S(2)}, u32[]{:S(2)}) collective-permute-start(f32[256,128]{1,0:T(8,128)} %get-tuple-element.18.own_g), channel_id=1, source_target_pairs={{1,0},{2,1},{3,2},{4,3},{5,4},{6,5},{7,6},{8,7},{9,8},{10,9},{11,1... | collective-permute-start | bytes 393224 | tf_op jit(solution)/shard_map/ppermute | solution.py:282
  138.7 1.9 %collective-permute-start.8 = (f32[768,128]{1,0:T(8,128)S(1)}, f32[768,128]{1,0:T(8,128)S(1)}, u32[]{:S(2)}, u32[]{:S(2)}) collective-permute-start(f32[768,128]{1,0:T(8,128)S(1)} %constant_dynamic-update-slice_fusion.5), channel_id=1, source_target_pairs={{384,0},{0,128},{128,256},{256,384},{385,1},{1,129},{129,257},{257... | collective-permute-start | bytes 1179656 | tf_op jit(solution)/shard_map/ppermute | solution.py:282
  140.7 3.9 %collective-permute-start.9 = (f32[768,128]{1,0:T(8,128)S(1)}, f32[768,128]{1,0:T(8,128)S(1)}, u32[]{:S(2)}, u32[]{:S(2)}) collective-permute-start(f32[768,128]{1,0:T(8,128)S(1)} %constant_dynamic-update-slice_fusion.5), channel_id=1, source_target_pairs={{128,0},{256,128},{384,256},{0,384},{129,1},{257,129},{385,257},{1... | collective-permute-start | bytes 1179656 | tf_op jit(solution)/shard_map/ppermute | solution.py:282
  144.6 3.8 %collective-permute-done.8 = f32[768,128]{1,0:T(8,128)S(1)} collective-permute-done((f32[768,128]{1,0:T(8,128)S(1)}, f32[768,128]{1,0:T(8,128)S(1)}, u32[]{:S(2)}, u32[]{:S(2)}) %collective-permute-start.8) | collective-permute-done | bytes 393248 | tf_op jit(solution)/shard_map/ppermute | solution.py:282
  148.6 1.8 collective-permute-done.9
  151.4 2.9 %tiles_to_send.3 = (f32[576,128]{1,0:T(8,128)}, f32[576,128]{1,0:T(8,128)}) custom-call(s32[36]{0:T(128)} %reshape.116.starts, f32[2304,128]{1,0:T(8,128)} %copy-done.2), custom_call_target="tpu_custom_call" | custom-call | tf_op jit(solution)/shard_map/tiles_to_send/pallas_call | solution.py:154
  154.3 1.9 collective-permute-start.10
  156.2 5.7 %collective-permute-start.11 = (f32[576,128]{1,0:T(8,128)}, f32[576,128]{1,0:T(8,128)S(1)}, u32[]{:S(2)}, u32[]{:S(2)}) collective-permute-start(f32[576,128]{1,0:T(8,128)} %get-tuple-element.20), channel_id=1, source_target_pairs={{96,0},{0,32},{32,64},{64,96},{97,1},{1,33},{33,65},{65,97},{98,2}... | collective-permute-start | bytes 884744 | tf_op jit(solution)/shard_map/ppermute | solution.py:282
  162.8 1.0 pad.31.r_near
  163.8 1.3 collective-permute-done.10
  165.1 3.0 %collective-permute-done.11 = f32[576,128]{1,0:T(8,128)S(1)} collective-permute-done((f32[576,128]{1,0:T(8,128)}, f32[576,128]{1,0:T(8,128)S(1)}, u32[]{:S(2)}, u32[]{:S(2)}) %collective-permute-start.11) | collective-permute-done | bytes 294944 | tf_op jit(solution)/shard_map/ppermute | solution.py:282
  168.1 1.2 copy-done.1
  169.3 21.3 %pair_gradients.1 = (f32[256,128]{1,0:T(8,128)}, f32[8,256]{1,0:T(8,128)}) custom-call(s32[1]{0:T(128)} %bitcast.14.count, s32[1792]{0:T(1024)} %fusion.26.order, s32[64]{0:T(128)} %pad.28.tiles, s32[64]{0:T(128)} %pad.29.starts, bf16[57344,128]{1,0:T(8,128)(2,1)} %get-tuple-element.13.filt, bf16[57344,128]{1,0:T(8,128)(2,1)} %get-tuple-element.17.filt_d, ...), custom_call_target="tpu_custom_call" | custom-call | tf_op jit(solution)/shard_map/pair_gradients/pallas_call | solution.py:265
  (134 shorter events, 21.3 us)
Async XLA Ops:
  0.6 39.0 %copy-start.20 = (s32[28]{0:T(128)S(1)}, s32[28]{0:T(128)}, u32[]{:S(2)}) copy-start(s32[28]{0:T(128)} %constant.128.clone) | copy-start | bytes 340
  0.6 39.0 %copy-start.21 = (s32[28]{0:T(128)S(1)}, s32[28]{0:T(128)}, u32[]{:S(2)}) copy-start(s32[28]{0:T(128)} %constant.127.clone) | copy-start | bytes 340
  0.7 39.0 %copy-start.22 = (s32[28]{0:T(128)S(1)}, s32[28]{0:T(128)}, u32[]{:S(2)}) copy-start(s32[28]{0:T(128)} %constant.126.clone) | copy-start | bytes 340
  4.0 42.7 %copy-start.4 = (f32[256,128]{1,0:T(8,128)}, f32[256,128]{1,0:T(8,128)S(1)}, u32[]{:S(2)}) copy-start(f32[256,128]{1,0:T(8,128)S(1)} %fusion.36.own_h) | copy-start | bytes 393220
  4.2 42.5 %copy-start.6 = (f32[46,392]{1,0:T(8,128)S(1)}, f32[46,392]{1,0:T(8,128)}, u32[]{:S(2)}) copy-start(f32[46,392]{1,0:T(8,128)} %constant.129.clone) | copy-start | bytes 216388
  4.2 43.0 %copy-start.19 = (pred[46]{0:T(512)(128)(4,1)S(1)}, pred[46]{0:T(512)(128)(4,1)}, u32[]{:S(2)}) copy-start(pred[46]{0:T(512)(128)(4,1)} %constant.169) | copy-start | bytes 142
  4.2 43.0 %copy-start.18 = (pred[28]{0:T(512)(128)(4,1)S(1)}, pred[28]{0:T(512)(128)(4,1)}, u32[]{:S(2)}) copy-start(pred[28]{0:T(512)(128)(4,1)} %constant.170) | copy-start | bytes 88
  4.2 15.3 %collective-permute-start.1 = (f32[1,264,128]{2,1,0:T(8,128)S(1)}, f32[1,264,128]{2,1,0:T(8,128)S(1)}, u32[]{:S(2)}, u32[]{:S(2)}) collective-permute-start(f32[1,264,128]{2,1,0:T(8,128)S(1)} %maximum_bitcast_fusion), channel_id=1, source_target_pairs={{1,0},{2,1},{3,2},{4,3},{5,4},{6,5},{7,6},{8,7},{9,8},{10,9},{11,1... | collective-permute-start | bytes 405512 | tf_op jit(solution)/shard_map/ppermute | solution.py:282
  17.0 12.3 %collective-permute-start = (f32[1,264,128]{2,1,0:T(8,128)S(1)}, f32[1,264,128]{2,1,0:T(8,128)S(1)}, u32[]{:S(2)}, u32[]{:S(2)}) collective-permute-start(f32[1,264,128]{2,1,0:T(8,128)S(1)} %maximum_bitcast_fusion), channel_id=1, source_target_pairs={{31,0},{0,1},{1,2},{2,3},{3,4},{4,5},{5,6},{6,7},{7,8},{8,9},{9,10... | collective-permute-start | bytes 405512 | tf_op jit(solution)/shard_map/ppermute | solution.py:282
  29.4 19.2 %copy-start.14 = (s32[28,2]{0,1:T(2,128)S(1)}, s32[28,2]{0,1:T(2,128)}, u32[]{:S(2)}) copy-start(s32[28,2]{0,1:T(2,128)} %constant.133.clone) | copy-start | bytes 676
  29.4 19.2 %copy-start.16 = (pred[28]{0:T(512)(128)(4,1)S(1)}, pred[28]{0:T(512)(128)(4,1)}, u32[]{:S(2)}) copy-start(pred[28]{0:T(512)(128)(4,1)} %constant.174) | copy-start | bytes 88
  29.4 19.2 %copy-start.17 = (s32[28]{0:T(128)S(1)}, s32[28]{0:T(128)}, u32[]{:S(2)}) copy-start(s32[28]{0:T(128)} %constant.175) | copy-start | bytes 340
  29.4 19.4 %copy-start.5 = (f32[56,1792]{1,0:T(8,128)S(1)}, f32[56,1792]{1,0:T(8,128)}, u32[]{:S(2)}) copy-start(f32[56,1792]{1,0:T(8,128)} %constant.137.clone) | copy-start | bytes 1204228
  30.1 15.5 %all-to-all-start = ((f32[16,24,128]{2,1,0:T(8,128)}), f32[16,24,128]{2,1,0:T(8,128)S(1)}, u32[]{:S(2)}, u32[]{:S(2)}) async-start(f32[16,24,128]{2,1,0:T(8,128)} %broadcast_in_dim.100), calls=%async_computation | async-start | bytes 393216 | tf_op jit(solution)/shard_map/all_to_all | solution.py:335
  39.7 53.4 %collective-permute-start.2 = (f32[768,128]{1,0:T(8,128)S(1)}, f32[768,128]{1,0:T(8,128)S(1)}, u32[]{:S(2)}, u32[]{:S(2)}) collective-permute-start(f32[768,128]{1,0:T(8,128)S(1)} %bitcast.70), channel_id=1, source_target_pairs={{384,0},{0,128},{128,256},{256,384},{385,1},{1,129},{129,257},{257... | collective-permute-start | bytes 1179656 | tf_op jit(solution)/shard_map/ppermute | solution.py:282
  43.1 50.0 %collective-permute-start.3 = (f32[768,128]{1,0:T(8,128)S(1)}, f32[768,128]{1,0:T(8,128)S(1)}, u32[]{:S(2)}, u32[]{:S(2)}) collective-permute-start(f32[768,128]{1,0:T(8,128)S(1)} %bitcast.71), channel_id=1, source_target_pairs={{128,0},{256,128},{384,256},{0,384},{129,1},{257,129},{385,257},{1... | collective-permute-start | bytes 1179656 | tf_op jit(solution)/shard_map/ppermute | solution.py:282
  45.9 4.3 %copy-start.8 = (f32[56,3]{1,0:T(8,128)S(1)}, f32[56,3]{1,0:T(8,128)}, u32[]{:S(2)}) copy-start(f32[56,3]{1,0:T(8,128)} %constant.172) | copy-start | bytes 2020
  51.1 2.6 %copy-start.7 = (f32[128,128]{1,0:T(8,128)S(1)}, f32[128,128]{1,0:T(8,128)}, u32[]{:S(2)}) copy-start(f32[128,128]{1,0:T(8,128)} %constant.141.clone) | copy-start | bytes 196612
  51.1 3.0 %copy-start.10 = (f32[14,14]{1,0:T(8,128)S(1)}, f32[14,14]{1,0:T(8,128)}, u32[]{:S(2)}) copy-start(f32[14,14]{1,0:T(8,128)} %constant.142.clone) | copy-start | bytes 2356
  51.1 6.2 %copy-start.15 = (s32[18]{0:T(128)S(1)}, s32[18]{0:T(128)}, u32[]{:S(2)}) copy-start(s32[18]{0:T(128)} %constant.176) | copy-start | bytes 220
  97.1 10.7 %collective-permute-start.4 = (f32[576,128]{1,0:T(8,128)}, f32[576,128]{1,0:T(8,128)S(1)}, u32[]{:S(2)}, u32[]{:S(2)}) collective-permute-start(f32[576,128]{1,0:T(8,128)} %get-tuple-element.14), channel_id=1, source_target_pairs={{32,0},{64,32},{96,64},{0,96},{33,1},{65,33},{97,65},{1,97},{34,2}... | collective-permute-start | bytes 884744 | tf_op jit(solution)/shard_map/ppermute | solution.py:282
  99.0 11.9 %collective-permute-start.5 = (f32[576,128]{1,0:T(8,128)}, f32[576,128]{1,0:T(8,128)S(1)}, u32[]{:S(2)}, u32[]{:S(2)}) collective-permute-start(f32[576,128]{1,0:T(8,128)} %get-tuple-element.15), channel_id=1, source_target_pairs={{96,0},{0,32},{32,64},{64,96},{97,1},{1,33},{33,65},{65,97},{98,2}... | collective-permute-start | bytes 884744 | tf_op jit(solution)/shard_map/ppermute | solution.py:282
  110.8 1.2 copy-start
  124.2 24.3 %copy-start.3 = (f32[256,128]{1,0:T(8,128)S(1)}, f32[256,128]{1,0:T(8,128)}, u32[]{:S(2)}) copy-start(f32[256,128]{1,0:T(8,128)} %get-tuple-element.18.own_g) | copy-start | bytes 393220
  124.2 12.6 %collective-permute-start.6 = (f32[256,128]{1,0:T(8,128)}, f32[256,128]{1,0:T(8,128)S(1)}, u32[]{:S(2)}, u32[]{:S(2)}) collective-permute-start(f32[256,128]{1,0:T(8,128)} %get-tuple-element.18.own_g), channel_id=1, source_target_pairs={{31,0},{0,1},{1,2},{2,3},{3,4},{4,5},{5,6},{6,7},{7,8},{8,9},{9,10... | collective-permute-start | bytes 393224 | tf_op jit(solution)/shard_map/ppermute | solution.py:282
  126.2 12.5 %collective-permute-start.7 = (f32[256,128]{1,0:T(8,128)}, f32[256,128]{1,0:T(8,128)S(1)}, u32[]{:S(2)}, u32[]{:S(2)}) collective-permute-start(f32[256,128]{1,0:T(8,128)} %get-tuple-element.18.own_g), channel_id=1, source_target_pairs={{1,0},{2,1},{3,2},{4,3},{5,4},{6,5},{7,6},{8,7},{9,8},{10,9},{11,1... | collective-permute-start | bytes 393224 | tf_op jit(solution)/shard_map/ppermute | solution.py:282
  138.7 9.7 %collective-permute-start.8 = (f32[768,128]{1,0:T(8,128)S(1)}, f32[768,128]{1,0:T(8,128)S(1)}, u32[]{:S(2)}, u32[]{:S(2)}) collective-permute-start(f32[768,128]{1,0:T(8,128)S(1)} %constant_dynamic-update-slice_fusion.5), channel_id=1, source_target_pairs={{384,0},{0,128},{128,256},{256,384},{385,1},{1,129},{129,257},{257... | collective-permute-start | bytes 1179656 | tf_op jit(solution)/shard_map/ppermute | solution.py:282
  140.7 9.7 %collective-permute-start.9 = (f32[768,128]{1,0:T(8,128)S(1)}, f32[768,128]{1,0:T(8,128)S(1)}, u32[]{:S(2)}, u32[]{:S(2)}) collective-permute-start(f32[768,128]{1,0:T(8,128)S(1)} %constant_dynamic-update-slice_fusion.5), channel_id=1, source_target_pairs={{128,0},{256,128},{384,256},{0,384},{129,1},{257,129},{385,257},{1... | collective-permute-start | bytes 1179656 | tf_op jit(solution)/shard_map/ppermute | solution.py:282
  148.5 13.5 %copy-start.9 = (f32[1,1,1,3,256]{4,2,3,1,0:T(1,128)S(1)}, f32[1,1,1,3,256]{4,2,3,1,0:T(1,128)}, u32[]{:S(2)}) copy-start(f32[1,1,1,3,256]{4,2,3,1,0:T(1,128)} %param.36) | copy-start | bytes 9220
  154.3 10.8 %collective-permute-start.10 = (f32[576,128]{1,0:T(8,128)}, f32[576,128]{1,0:T(8,128)S(1)}, u32[]{:S(2)}, u32[]{:S(2)}) collective-permute-start(f32[576,128]{1,0:T(8,128)} %get-tuple-element.19), channel_id=1, source_target_pairs={{32,0},{64,32},{96,64},{0,96},{33,1},{65,33},{97,65},{1,97},{34,2}... | collective-permute-start | bytes 884744 | tf_op jit(solution)/shard_map/ppermute | solution.py:282
  156.2 11.9 %collective-permute-start.11 = (f32[576,128]{1,0:T(8,128)}, f32[576,128]{1,0:T(8,128)S(1)}, u32[]{:S(2)}, u32[]{:S(2)}) collective-permute-start(f32[576,128]{1,0:T(8,128)} %get-tuple-element.20), channel_id=1, source_target_pairs={{96,0},{0,32},{32,64},{64,96},{97,1},{1,33},{33,65},{65,97},{98,2}... | collective-permute-start | bytes 884744 | tf_op jit(solution)/shard_map/ppermute | solution.py:282
  168.1 1.2 copy-start.1
  (4 other events, 3.4 us)
where the time goes:
time: 193 us; the launch traced here: 192 us
  Pallas kernels  72.4 us (38%)
  starting transfers between devices  61.2 us (32%)
  waiting for transfers between devices  28.1 us (15%)
  local copies, waits for them, and re-layouts  14.8 us (8%)
  other arithmetic  10 us (5%)
  matrix products  2.74 us (1%)
  between operations  2.6 us (1%)
    ppermute x12, starting transfers between devices, moved(): return lax.ppermute(x, axis, [((i + by) % size, i) for i in range(size)])  53.3 us
    pallas_call x2, Pallas kernels, pair_call(): pl.pallas_call(body, grid_spec=pltpu.PrefetchScalarGridSpec(num_scalar_pr...  33.4 us
    pallas_call x1, Pallas kernels, filters(): pl.pallas_call(filter_kernel, grid_spec=pltpu.PrefetchScalarGridSpec(num_...  33.3 us
    ppermute x12, waiting for transfers between devices, moved(): return lax.ppermute(x, axis, [((i + by) % size, i) for i in range(size)])  28.1 us
    all_to_all x1, starting transfers between devices, on_device(): lax.all_to_all(jnp.broadcast_to(meta_three.reshape(1, 24, 128), (along *...  7.85 us
    unnamed x60, local copies, waits for them, and re-layouts  6.21 us
    pallas_call x2, Pallas kernels, gather_tiles(): pl.pallas_call(gather_kernel, grid_spec=pltpu.PrefetchScalarGridSpec(num_...  5.75 us
  transfers between devices with their start and end apart: 13, of which 10 were waited for; matrix products, arithmetic and copies ran while one was open for 9% of the time, Pallas kernels for 17%

commit v1 on v0

--- a/solution.py
+++ b/solution.py
@@ -68,11 +68,13 @@
     return jnp.dot(a, b, precision=lax.Precision.HIGHEST)
 
 
-BODY = 16
+BODY = 64
 ROWS = BODY * TILE
 SLABS = UNITS * TILE
+NINE = 9 * 256
+AROUND_ROWS = NINE + 2 * 18 * TILE
 BODIES = SLABS // BODY
-STEP = 8
+STEP = 2
 STEPS = BODIES // STEP
 
 
@@ -103,7 +105,7 @@
         z = 1.0 + jnp.exp(first[:, 0:128] + first_b[...])
         act = jnp.log(z) - LOG_TWO
         deriv = first[:, 128:256]
-        deriv = deriv - deriv * pl.reciprocal(z, approx=True)
+        deriv = deriv - deriv * pltpu.reciprocal(z, approx=True)
         both2 = jnp.concatenate([act.astype(jnp.bfloat16), deriv.astype(jnp.bfloat16)], axis=1)
         second = jnp.dot(both2, second_w[...], preferred_element_type=jnp.float32)
         base = second[:, 0:128] + second_b[...]
@@ -136,33 +138,43 @@
     )(count, order, *arrays)
 
 
-def gather_kernel(starts, table, up, down):
+def laid_end_to_end(pieces, held):
+    row = 0
+    for piece in pieces:
+        held[row : row + piece.shape[0], :] = piece[...]
+        row += piece.shape[0]
+
+
+def gather_kernel(starts, one_side, middle, other_side, near, far, held):
+    laid_end_to_end((one_side, middle, other_side), held)
+
     def one(index, carry):
         a = pl.multiple_of(starts[index], TILE)
         b = pl.multiple_of(starts[18 + index], TILE)
         o = pl.multiple_of(index * TILE, TILE)
-        up[pl.ds(o, TILE), :] = table[pl.ds(a, TILE), :]
-        down[pl.ds(o, TILE), :] = table[pl.ds(b, TILE), :]
+        near[pl.ds(o, TILE), :] = held[pl.ds(a, TILE), :]
+        far[pl.ds(o, TILE), :] = held[pl.ds(b, TILE), :]
         return carry
 
     lax.fori_loop(0, 18, one, 0)
 
 
-def gather_tiles(starts, table):
+def gather_tiles(starts, pieces):
     shape = (18 * TILE, 128)
-    whole = pl.BlockSpec(shape, lambda s, *_: (0, 0))
+    outs = [jax.ShapeDtypeStruct(shape, jnp.float32)] * 2
     return pl.pallas_call(
         gather_kernel,
         grid_spec=pltpu.PrefetchScalarGridSpec(
             num_scalar_prefetch=1,
             grid=(1,),
-            in_specs=[pl.BlockSpec(table.shape, lambda s, *_: (0, 0))],
-            out_specs=[whole, whole],
+            in_specs=[whole(p) for p in pieces],
+            out_specs=[whole(o) for o in outs],
+            scratch_shapes=[pltpu.VMEM((NINE, 128), jnp.float32)],
         ),
-        out_shape=[jax.ShapeDtypeStruct(shape, jnp.float32)] * 2,
+        out_shape=outs,
         compiler_params=pltpu.CompilerParams(vmem_limit_bytes=VMEM),
         name="tiles_to_send",
-    )(starts, table)
+    )(starts, *pieces)
 
 
 def softplus(values):
@@ -177,12 +189,14 @@
 
 
 def message_kernel(
-    count, order, tiles, starts, filt, near, feats, cot, out_w, out_b, fin_w, fin_b, new, grad, *totals
+    count, order, tiles, starts, filt, p0, p1, p2, p3, p4, feats, cot, out_w, out_b, fin_w, fin_b,
+    new, grad, near, *totals
 ):
     step = pl.program_id(0)
 
     @pl.when(step == 0)
     def _():
+        laid_end_to_end((p0, p1, p2, p3, p4), near)
         for total in totals:
             total[...] = jnp.zeros_like(total)
 
@@ -212,8 +226,8 @@
 
 
 def back_kernel(
-    count, order, tiles, starts, filt, filt_d, near, g_near, own_h, own_g, r_near, r_own, cot, in_w,
-    grad, force, *totals
+    count, order, tiles, starts, filt, filt_d, h0, h1, h2, h3, h4, g0, g1, g2, g3, g4, own_h, own_g,
+    r_near, r_own, cot, in_w, grad, force, near, g_near, *totals
 ):
     step = pl.program_id(0)
     pushes = totals[CHAINS:]
@@ -221,6 +235,8 @@
 
     @pl.when(step == 0)
     def _():
+        laid_end_to_end((h0, h1, h2, h3, h4), near)
+        laid_end_to_end((g0, g1, g2, g3, g4), g_near)
         for total in (*totals, *pushes):
             total[...] = jnp.zeros_like(total)
 
@@ -260,7 +276,7 @@
         force[...] = sum(push[...] for push in pushes).T[0:8, :]
 
 
-def pair_call(body, scalars, streams, arrays, outs, scratch, name):
+def pair_call(body, scalars, streams, arrays, outs, tables, scratch, name):
     stream = pl.BlockSpec((STEP * ROWS, 128), lambda s, n, *_: (last_block(s, n), 0))
     return pl.pallas_call(
         body,
@@ -269,7 +285,8 @@
             grid=(STEPS,),
             in_specs=[stream] * len(streams) + [whole(a) for a in arrays],
             out_specs=[whole(o) for o in outs],
-            scratch_shapes=[pltpu.VMEM((256, 128), jnp.float32)] * scratch,
+            scratch_shapes=[pltpu.VMEM((AROUND_ROWS, 128), jnp.float32)] * tables
+            + [pltpu.VMEM((256, 128), jnp.float32)] * scratch,
         ),
         out_shape=outs,
         compiler_params=pltpu.CompilerParams(vmem_limit_bytes=VMEM),
@@ -277,22 +294,26 @@
     )(*scalars, *streams, *arrays)
 
 
-def moved(x, axis, by):
+def swapped(to_far, to_near, axis):
     size = lax.axis_size(axis)
-    return lax.ppermute(x, axis, [((i + by) % size, i) for i in range(size)])
+    near = [(i, i ^ 1) for i in range(size)]
+    far = [(i, ((i ^ 1) + 2 * (2 * (i % 2) - 1)) % size) for i in range(size)]
+    from_far = lax.ppermute(to_far, axis, far)
+    return lax.ppermute(to_near, axis, near), from_far
+
+
+def place_of(steps, axis):
+    return 1 - steps * (1 - 2 * (lax.axis_index(axis) % 2))
 
 
 def planes(own):
-    return jnp.concatenate([moved(own, "gz", -1), own, moved(own, "gz", 1)], axis=0)
+    near, far = swapped(own, own, "gz")
+    return jnp.concatenate([near, own, far], axis=0)
 
 
 def columns(three):
-    return jnp.concatenate([moved(three, "gx", -1), three, moved(three, "gx", 1)], axis=0)
-
-
-def rows_around(nine, wanted):
-    to_lower, to_upper = gather_tiles(wanted, nine)
-    return jnp.concatenate([nine, moved(to_lower, "gy", 1), moved(to_upper, "gy", -1)], axis=0)
+    near, far = swapped(three, three, "gx")
+    return [near, three, far]
 
 
 def block_diagonal(weight):
@@ -341,7 +362,8 @@
     everyone = everyone.reshape(along * across * 3, 8 * 128)
     side = np.array(SLOTS)
     holders = (lax.axis_index("gx") + side[:, 0]) % along * across
-    holders = (holders + (lax.axis_index("gy") + side[:, 1]) % across) * 3 + side[:, 2] + 1
+    holders = (holders + (lax.axis_index("gy") + side[:, 1]) % across) * 3
+    holders = holders + place_of(side[:, 2], "gz")
     picker = (holders[:, None] == jnp.arange(along * across * 3)[None, :]).astype(jnp.float32)
     slots = exact_dot(picker, everyone)
 
@@ -351,14 +373,20 @@
     mine = jnp.where(forward, lists[:, 0:2], lists[:, 2:4])
     theirs = jnp.where(forward, lists[:, 2:4], lists[:, 0:2])
     own_tiles, other_tiles = mine[:28], theirs[:28]
-    column = ((side[:, 0] + 1) * 3 + side[:, 2] + 1)[:, None]
+    column = (place_of(side[:, 0], "gx") * 3 + place_of(side[:, 2], "gz"))[:, None]
+    listed = ((side[:, 0] + 1) * 3 + side[:, 2] + 1)[:, None]
     entry = np.arange(2)[None]
     starts = jnp.where(
         (side[:, 1] == 0)[:, None],
         column * 256 + other_tiles * TILE,
-        2304 + 576 * (side[:, 1:2] < 0) + (column * 2 + entry) * TILE,
-    )
-    wanted = (np.tile(np.arange(9), 2)[:, None] * 256 + theirs[28:] * TILE).reshape(36)
+        NINE + 288 * place_of(side[:, 1:2], "gy") + (listed * 2 + entry) * TILE,
+    )
+    sent = np.array([(sx, sz) for sx in (-1, 0, 1) for sz in (-1, 0, 1)])
+    sent_column = (place_of(sent[:, 0], "gx") * 3 + place_of(sent[:, 1], "gz"))[:, None]
+    wanted = sent_column * 256 + theirs[28:].reshape(2, 9, 2) * TILE
+    lower, upper = wanted[0].reshape(18), wanted[1].reshape(18)
+    even = lax.axis_index("gy") % 2 == 0
+    wanted = jnp.concatenate([jnp.where(even, upper, lower), jnp.where(even, lower, upper)])
 
     pick_other = (other_tiles[:, :, None] == jnp.arange(8)).astype(jnp.float32)
     slot_pos = slots[:, : 6 * 128].reshape(28, 1, 3, 8, TILE)
@@ -405,6 +433,9 @@
     order = jnp.where(slab < total, order, SLABS).astype(jnp.int32)
     count = ((total + BODY - 1) // BODY).reshape(1)
 
+    near_x = columns(hidden_three)
+    to_near, to_far, count = lax.optimization_barrier((*gather_tiles(wanted, near_x), count))
+    near = [*near_x, *swapped(to_far, to_near, "gy")]
     filt, filt_d = filters(
         count,
         order,
@@ -414,7 +445,6 @@
         radial_bias[None],
         filter_bias[None],
     )
-    near = rows_around(columns(hidden_three), wanted)
     cot = cotangent.reshape(256, 128)
     scalars = (
         count,
@@ -427,7 +457,7 @@
         scalars,
         [filt],
         [
-            near,
+            *near,
             own_features,
             cot,
             output_weight,
@@ -439,21 +469,25 @@
             jax.ShapeDtypeStruct((256, 128), jnp.bfloat16),
             jax.ShapeDtypeStruct((256, 128), jnp.float32),
         ],
+        1,
         CHAINS,
         "messages_and_update",
     )
-    g_near = rows_around(columns(planes(d_msg)), wanted)
+    g_x = columns(planes(d_msg))
+    to_near, to_far = gather_tiles(wanted, g_x)
+    g_near = [*g_x, *swapped(to_far, to_near, "gy")]
     r_near = jnp.pad(other_at.transpose(0, 2, 1).reshape(SLABS, 3), ((0, 8), (0, 125)))
     r_own = jnp.pad(own_pos.T, ((0, 0), (0, 125)))
     grad_features, force = pair_call(
         back_kernel,
         scalars,
         [filt, filt_d],
-        [near, g_near, hidden, d_msg, r_near, r_own, cot, input_weight],
+        [*near, *g_near, hidden, d_msg, r_near, r_own, cot, input_weight],
         [
             jax.ShapeDtypeStruct((256, 128), jnp.float32),
             jax.ShapeDtypeStruct((8, 256), jnp.float32),
         ],
+        2,
         2 * CHAINS,
         "pair_gradients",
     )

time: 193 us -> 174 us (0.902)
  the two profiles are of different devices: /device:TPU:58 before, /device:TPU:12 now
where the time goes in v1:
time: 174 us; the launch traced here: 172 us
  Pallas kernels  59.5 us (34%)
  starting transfers between devices  50.7 us (29%)
  waiting for transfers between devices  25.6 us (15%)
  other arithmetic  15 us (9%)
  local copies, waits for them, and re-layouts  14.4 us (8%)
  matrix products  4.64 us (3%)
  between operations  2.48 us (1%)
    ppermute x6, starting transfers between devices, swapped(): from_far = lax.ppermute(to_far, axis, far)  29.8 us
    pallas_call x2, Pallas kernels, pair_call(): pl.pallas_call(body, grid_spec=pltpu.PrefetchScalarGridSpec(num_scalar_pr...  29.4 us
    pallas_call x1, Pallas kernels, filters(): pl.pallas_call(filter_kernel, grid_spec=pltpu.PrefetchScalarGridSpec(num_...  24.3 us
    ppermute x6, waiting for transfers between devices, swapped(): from_far = lax.ppermute(to_far, axis, far)  19.9 us
    ppermute x6, starting transfers between devices, swapped(): return (lax.ppermute(to_near, axis, near), from_far)  14.2 us
    all_to_all x1, starting transfers between devices, on_device(): lax.all_to_all(jnp.broadcast_to(meta_three.reshape(1, 24, 128), (along *...  6.76 us
    unnamed x37, local copies, waits for them, and re-layouts  6.22 us
    pallas_call x2, Pallas kernels, gather_tiles(): pl.pallas_call(gather_kernel, grid_spec=pltpu.PrefetchScalarGridSpec(num_...  5.82 us
  transfers between devices with their start and end apart: 13, of which 5 were waited for; matrix products, arithmetic and copies ran while one was open for 15% of the time, Pallas kernels for 14%

profile of v1, /device:TPU:12, one launch (start us, length us, event | category | flops | bytes accessed | tf_op | source)
XLA Modules:
  0.0 172.4 jit_solution(1310359890149234635)
XLA Ops:
  3.1 1.0 fusion.35.own_h
  4.2 14.7 %collective-permute-start.1 = (f32[1,264,128]{2,1,0:T(8,128)S(1)}, f32[1,264,128]{2,1,0:T(8,128)S(1)}, u32[]{:S(2)}, u32[]{:S(2)}) collective-permute-start(f32[1,264,128]{2,1,0:T(8,128)S(1)} %maximum_bitcast_fusion), channel_id=1, source_target_pairs={{0,31},{1,2},{2,1},{3,4},{4,3},{5,6},{6,5},{7,8},{8,7},{9,10},{10,... | collective-permute-start | bytes 405512 | tf_op jit(solution)/shard_map/ppermute | solution.py:301
  19.0 1.9 %collective-permute-start = (f32[1,264,128]{2,1,0:T(8,128)S(1)}, f32[1,264,128]{2,1,0:T(8,128)S(1)}, u32[]{:S(2)}, u32[]{:S(2)}) collective-permute-start(f32[1,264,128]{2,1,0:T(8,128)S(1)} %maximum_bitcast_fusion), channel_id=1, source_target_pairs={{0,1},{1,0},{2,3},{3,2},{4,5},{5,4},{6,7},{7,6},{8,9},{9,8},{10,11... | collective-permute-start | bytes 405512 | tf_op jit(solution)/shard_map/ppermute | solution.py:302
  23.0 6.8 %all-to-all-start = ((f32[16,24,128]{2,1,0:T(8,128)}), f32[16,24,128]{2,1,0:T(8,128)S(1)}, u32[]{:S(2)}, u32[]{:S(2)}) async-start(f32[16,24,128]{2,1,0:T(8,128)} %broadcast_in_dim.103), calls=%async_computation | async-start | bytes 393216 | tf_op jit(solution)/shard_map/all_to_all | solution.py:356
  29.8 1.6 fusion.18
  32.2 2.5 %collective-permute-start.3 = (f32[768,128]{1,0:T(8,128)S(1)}, f32[768,128]{1,0:T(8,128)S(1)}, u32[]{:S(2)}, u32[]{:S(2)}) collective-permute-start(f32[768,128]{1,0:T(8,128)S(1)} %bitcast.74), channel_id=1, source_target_pairs={{0,384},{128,256},{256,128},{384,0},{1,385},{129,257},{257,129},{3... | collective-permute-start | bytes 1179656 | tf_op jit(solution)/shard_map/ppermute | solution.py:301
  34.7 3.1 %collective-permute-start.2 = (f32[768,128]{1,0:T(8,128)S(1)}, f32[768,128]{1,0:T(8,128)S(1)}, u32[]{:S(2)}, u32[]{:S(2)}) collective-permute-start(f32[768,128]{1,0:T(8,128)S(1)} %bitcast.75), channel_id=1, source_target_pairs={{0,128},{128,0},{256,384},{384,256},{1,129},{129,1},{257,385},{385... | collective-permute-start | bytes 1179656 | tf_op jit(solution)/shard_map/ppermute | solution.py:302
  39.0 1.3 fusion.2
  44.1 1.3 fusion.27
  48.9 1.0 multiply_select_fusion
  52.9 1.5 fusion
  56.0 2.9 %tiles_to_send.2 = (f32[576,128]{1,0:T(8,128)}, f32[576,128]{1,0:T(8,128)}) custom-call(s32[36]{0:T(128)} %pad_add_fusion.starts, f32[768,128]{1,0:T(8,128)} %copy-done.2, f32[768,128]{1,0:T(8,128)} %bitcast.76, f32[768,128]{1,0:T(8,128)} %copy-done.1), custom_call_target="tpu_custom_call" | custom-call | tf_op jit(solution)/shard_map/tiles_to_send/pallas_call | solution.py:165
  58.9 2.0 %collective-permute-start.4 = (f32[576,128]{1,0:T(8,128)}, f32[576,128]{1,0:T(8,128)S(1)}, u32[]{:S(2)}, u32[]{:S(2)}) collective-permute-start(f32[576,128]{1,0:T(8,128)} %get-tuple-element.20), channel_id=1, source_target_pairs={{0,32},{32,0},{64,96},{96,64},{1,33},{33,1},{65,97},{97,65},{2,34}... | collective-permute-start | bytes 884744 | tf_op jit(solution)/shard_map/ppermute | solution.py:302
  60.9 4.7 %collective-permute-start.5 = (f32[576,128]{1,0:T(8,128)}, f32[576,128]{1,0:T(8,128)S(1)}, u32[]{:S(2)}, u32[]{:S(2)}) collective-permute-start(f32[576,128]{1,0:T(8,128)} %get-tuple-element.21), channel_id=1, source_target_pairs={{0,96},{32,64},{64,32},{96,0},{1,97},{33,65},{65,33},{97,1},{2,98}... | collective-permute-start | bytes 884744 | tf_op jit(solution)/shard_map/ppermute | solution.py:301
  67.7 1.0 select_maximum_fusion.table
  68.7 24.3 %pair_filters.1 = (bf16[57344,128]{1,0:T(8,128)(2,1)}, bf16[57344,128]{1,0:T(8,128)(2,1)}) custom-call(s32[1]{0:T(128)} %bitcast.15.count, s32[1792]{0:T(1024)} %fusion.26.order, f32[128,1920]{1,0:T(8,128)} %select_maximum_fusion.table, f32[1,128]{1,0:T(1,128)} %constant.187.clone.centres, bf16[256,256]{1,0:T(8,128)(2,1)} %get-tuple-element.62.first_w, ...), custom_call_target="tpu_custom_call" | custom-call | tf_op jit(solution)/shard_map/pair_filters/pallas_call | solution.py:127
  93.8 11.8 %messages_and_update.1 = (bf16[256,128]{1,0:T(8,128)(2,1)}, f32[256,128]{1,0:T(8,128)}) custom-call(s32[1]{0:T(128)} %bitcast.15.count, s32[1792]{0:T(1024)} %fusion.26.order, s32[64]{0:T(128)} %pad.28.tiles, s32[64]{0:T(128)} %pad.29.starts, bf16[57344,128]{1,0:T(8,128)(2,1)} %get-tuple-element.19.filt, f32[768,128]{1,0:T(8,128)} %copy-done.2, ...), custom_call_target="tpu_custom_call" | custom-call | tf_op jit(solution)/shard_map/messages_and_update/pallas_call | solution.py:281
  105.6 1.9 %collective-permute-start.6 = (f32[256,128]{1,0:T(8,128)}, f32[256,128]{1,0:T(8,128)S(1)}, u32[]{:S(2)}, u32[]{:S(2)}) collective-permute-start(f32[256,128]{1,0:T(8,128)} %get-tuple-element.24.own_g), channel_id=1, source_target_pairs={{0,1},{1,0},{2,3},{3,2},{4,5},{5,4},{6,7},{7,6},{8,9},{9,8},{10,11... | collective-permute-start | bytes 393224 | tf_op jit(solution)/shard_map/ppermute | solution.py:302
  107.6 1.9 %collective-permute-start.7 = (f32[256,128]{1,0:T(8,128)}, f32[256,128]{1,0:T(8,128)S(1)}, u32[]{:S(2)}, u32[]{:S(2)}) collective-permute-start(f32[256,128]{1,0:T(8,128)} %get-tuple-element.24.own_g), channel_id=1, source_target_pairs={{0,31},{1,2},{2,1},{3,4},{4,3},{5,6},{6,5},{7,8},{8,7},{9,10},{10,... | collective-permute-start | bytes 393224 | tf_op jit(solution)/shard_map/ppermute | solution.py:301
  109.5 0.9 constant_dynamic-update-slice_fusion.1
  110.4 9.6 %collective-permute-done.7 = f32[256,128]{1,0:T(8,128)S(1)} collective-permute-done((f32[256,128]{1,0:T(8,128)}, f32[256,128]{1,0:T(8,128)S(1)}, u32[]{:S(2)}, u32[]{:S(2)}) %collective-permute-start.7) | collective-permute-done | bytes 131104 | tf_op jit(solution)/shard_map/ppermute | solution.py:301
  120.1 4.0 %collective-permute-start.9 = (f32[768,128]{1,0:T(8,128)S(1)}, f32[768,128]{1,0:T(8,128)S(1)}, u32[]{:S(2)}, u32[]{:S(2)}) collective-permute-start(f32[768,128]{1,0:T(8,128)S(1)} %constant_dynamic-update-slice_fusion.middle.g1), channel_id=1, source_target_pairs={{0,384},{128,256},{256,128},{384,0},{1,385},{129,257},{257,129},{3... | collective-permute-start | bytes 1179656 | tf_op jit(solution)/shard_map/ppermute | solution.py:301
  124.1 1.9 %collective-permute-start.8 = (f32[768,128]{1,0:T(8,128)S(1)}, f32[768,128]{1,0:T(8,128)S(1)}, u32[]{:S(2)}, u32[]{:S(2)}) collective-permute-start(f32[768,128]{1,0:T(8,128)S(1)} %constant_dynamic-update-slice_fusion.middle.g1), channel_id=1, source_target_pairs={{0,128},{128,0},{256,384},{384,256},{1,129},{129,1},{257,385},{385... | collective-permute-start | bytes 1179656 | tf_op jit(solution)/shard_map/ppermute | solution.py:302
  126.1 3.8 %collective-permute-done.9.other_side.g2 = f32[768,128]{1,0:T(8,128)S(1)} collective-permute-done((f32[768,128]{1,0:T(8,128)S(1)}, f32[768,128]{1,0:T(8,128)S(1)}, u32[]{:S(2)}, u32[]{:S(2)}) %collective-permute-start.9) | collective-permute-done | bytes 393248 | tf_op jit(solution)/shard_map/ppermute | solution.py:301
  129.9 3.9 %collective-permute-done.8.one_side.g0 = f32[768,128]{1,0:T(8,128)S(1)} collective-permute-done((f32[768,128]{1,0:T(8,128)S(1)}, f32[768,128]{1,0:T(8,128)S(1)}, u32[]{:S(2)}, u32[]{:S(2)}) %collective-permute-start.8) | collective-permute-done | bytes 393248 | tf_op jit(solution)/shard_map/ppermute | solution.py:302
  134.5 2.9 %tiles_to_send.3 = (f32[576,128]{1,0:T(8,128)}, f32[576,128]{1,0:T(8,128)}) custom-call(s32[36]{0:T(128)} %pad_add_fusion.starts, f32[768,128]{1,0:T(8,128)} %copy-done.5, f32[768,128]{1,0:T(8,128)} %copy-done.3, f32[768,128]{1,0:T(8,128)} %copy-done.4), custom_call_target="tpu_custom_call" | custom-call | tf_op jit(solution)/shard_map/tiles_to_send/pallas_call | solution.py:165
  137.4 3.3 %collective-permute-start.10 = (f32[576,128]{1,0:T(8,128)}, f32[576,128]{1,0:T(8,128)S(1)}, u32[]{:S(2)}, u32[]{:S(2)}) collective-permute-start(f32[576,128]{1,0:T(8,128)} %get-tuple-element.25), channel_id=1, source_target_pairs={{0,32},{32,0},{64,96},{96,64},{1,33},{33,1},{65,97},{97,65},{2,34}... | collective-permute-start | bytes 884744 | tf_op jit(solution)/shard_map/ppermute | solution.py:302
  140.8 1.9 %collective-permute-start.11 = (f32[576,128]{1,0:T(8,128)}, f32[576,128]{1,0:T(8,128)S(1)}, u32[]{:S(2)}, u32[]{:S(2)}) collective-permute-start(f32[576,128]{1,0:T(8,128)} %get-tuple-element.26), channel_id=1, source_target_pairs={{0,96},{32,64},{64,32},{96,0},{1,97},{33,65},{65,33},{97,1},{2,98}... | collective-permute-start | bytes 884744 | tf_op jit(solution)/shard_map/ppermute | solution.py:301
  143.5 1.0 pad.31.r_near
  144.5 1.7 %collective-permute-done.10.g3 = f32[576,128]{1,0:T(8,128)S(1)} collective-permute-done((f32[576,128]{1,0:T(8,128)}, f32[576,128]{1,0:T(8,128)S(1)}, u32[]{:S(2)}, u32[]{:S(2)}) %collective-permute-start.10) | collective-permute-done | bytes 294944 | tf_op jit(solution)/shard_map/ppermute | solution.py:302
  146.3 6.5 %collective-permute-done.11.g4 = f32[576,128]{1,0:T(8,128)S(1)} collective-permute-done((f32[576,128]{1,0:T(8,128)}, f32[576,128]{1,0:T(8,128)S(1)}, u32[]{:S(2)}, u32[]{:S(2)}) %collective-permute-start.11) | collective-permute-done | bytes 294944 | tf_op jit(solution)/shard_map/ppermute | solution.py:301
  153.5 17.6 %pair_gradients.1 = (f32[256,128]{1,0:T(8,128)}, f32[8,256]{1,0:T(8,128)}) custom-call(s32[1]{0:T(128)} %bitcast.15.count, s32[1792]{0:T(1024)} %fusion.26.order, s32[64]{0:T(128)} %pad.28.tiles, s32[64]{0:T(128)} %pad.29.starts, bf16[57344,128]{1,0:T(8,128)(2,1)} %get-tuple-element.19.filt, bf16[57344,128]{1,0:T(8,128)(2,1)} %get-tuple-element.23.filt_d, ...), custom_call_target="tpu_custom_call" | custom-call | tf_op jit(solution)/shard_map/pair_gradients/pallas_call | solution.py:281
  (115 shorter events, 23.3 us)
Async XLA Ops:
  0.6 48.3 %copy-start.15 = (pred[1792]{0:T(1024)(128)(4,1)S(1)}, pred[1792]{0:T(1024)(128)(4,1)}, u32[]{:S(2)}) copy-start(pred[1792]{0:T(1024)(128)(4,1)} %constant.184.clone) | copy-start | bytes 5380
  0.6 48.3 %copy-start.14 = (f32[1792]{0:T(1024)S(1)}, f32[1792]{0:T(1024)}, u32[]{:S(2)}) copy-start(f32[1792]{0:T(1024)} %constant.183.clone) | copy-start | bytes 21508
  0.7 51.0 %copy-start.11 = (f32[128,128]{1,0:T(8,128)S(1)}, f32[128,128]{1,0:T(8,128)}, u32[]{:S(2)}) copy-start(f32[128,128]{1,0:T(8,128)} %constant.185.clone) | copy-start | bytes 196612
  0.7 51.4 %copy-start.13 = (f32[14,14]{1,0:T(8,128)S(1)}, f32[14,14]{1,0:T(8,128)}, u32[]{:S(2)}) copy-start(f32[14,14]{1,0:T(8,128)} %constant.186.clone) | copy-start | bytes 2356
  4.1 101.5 %copy-start.6 = (f32[256,128]{1,0:T(8,128)}, f32[256,128]{1,0:T(8,128)S(1)}, u32[]{:S(2)}) copy-start(f32[256,128]{1,0:T(8,128)S(1)} %fusion.35.own_h) | copy-start | bytes 393220
  4.2 18.1 %collective-permute-start.1 = (f32[1,264,128]{2,1,0:T(8,128)S(1)}, f32[1,264,128]{2,1,0:T(8,128)S(1)}, u32[]{:S(2)}, u32[]{:S(2)}) collective-permute-start(f32[1,264,128]{2,1,0:T(8,128)S(1)} %maximum_bitcast_fusion), channel_id=1, source_target_pairs={{0,31},{1,2},{2,1},{3,4},{4,3},{5,6},{6,5},{7,8},{8,7},{9,10},{10,... | collective-permute-start | bytes 405512 | tf_op jit(solution)/shard_map/ppermute | solution.py:301
  19.0 3.3 %collective-permute-start = (f32[1,264,128]{2,1,0:T(8,128)S(1)}, f32[1,264,128]{2,1,0:T(8,128)S(1)}, u32[]{:S(2)}, u32[]{:S(2)}) collective-permute-start(f32[1,264,128]{2,1,0:T(8,128)S(1)} %maximum_bitcast_fusion), channel_id=1, source_target_pairs={{0,1},{1,0},{2,3},{3,2},{4,5},{5,4},{6,7},{7,6},{8,9},{9,8},{10,11... | collective-permute-start | bytes 405512 | tf_op jit(solution)/shard_map/ppermute | solution.py:302
  23.0 14.8 %all-to-all-start = ((f32[16,24,128]{2,1,0:T(8,128)}), f32[16,24,128]{2,1,0:T(8,128)S(1)}, u32[]{:S(2)}, u32[]{:S(2)}) async-start(f32[16,24,128]{2,1,0:T(8,128)} %broadcast_in_dim.103), calls=%async_computation | async-start | bytes 393216 | tf_op jit(solution)/shard_map/all_to_all | solution.py:356
  32.2 22.3 %copy-start = (f32[3,256,128]{2,1,0:T(8,128)}, f32[3,256,128]{2,1,0:T(8,128)S(1)}, u32[]{:S(2)}) copy-start(f32[3,256,128]{2,1,0:T(8,128)S(1)} %pad_maximum_fusion) | copy-start | bytes 1179652
  32.2 22.2 %collective-permute-start.3 = (f32[768,128]{1,0:T(8,128)S(1)}, f32[768,128]{1,0:T(8,128)S(1)}, u32[]{:S(2)}, u32[]{:S(2)}) collective-permute-start(f32[768,128]{1,0:T(8,128)S(1)} %bitcast.74), channel_id=1, source_target_pairs={{0,384},{128,256},{256,128},{384,0},{1,385},{129,257},{257,129},{3... | collective-permute-start | bytes 1179656 | tf_op jit(solution)/shard_map/ppermute | solution.py:301
  34.7 19.8 %collective-permute-start.2 = (f32[768,128]{1,0:T(8,128)S(1)}, f32[768,128]{1,0:T(8,128)S(1)}, u32[]{:S(2)}, u32[]{:S(2)}) collective-permute-start(f32[768,128]{1,0:T(8,128)S(1)} %bitcast.75), channel_id=1, source_target_pairs={{0,128},{128,0},{256,384},{384,256},{1,129},{129,1},{257,385},{385... | collective-permute-start | bytes 1179656 | tf_op jit(solution)/shard_map/ppermute | solution.py:302
  48.8 93.9 %copy-start.12 = (f32[1,1,1,3,256]{4,2,3,1,0:T(1,128)S(1)}, f32[1,1,1,3,256]{4,2,3,1,0:T(1,128)}, u32[]{:S(2)}) copy-start(f32[1,1,1,3,256]{4,2,3,1,0:T(1,128)} %param.39) | copy-start | bytes 9220
  54.5 0.8 copy-start.1
  55.2 0.7 copy-start.2
  58.9 34.1 %collective-permute-start.4 = (f32[576,128]{1,0:T(8,128)}, f32[576,128]{1,0:T(8,128)S(1)}, u32[]{:S(2)}, u32[]{:S(2)}) collective-permute-start(f32[576,128]{1,0:T(8,128)} %get-tuple-element.20), channel_id=1, source_target_pairs={{0,32},{32,0},{64,96},{96,64},{1,33},{33,1},{65,97},{97,65},{2,34}... | collective-permute-start | bytes 884744 | tf_op jit(solution)/shard_map/ppermute | solution.py:302
  60.9 32.1 %collective-permute-start.5 = (f32[576,128]{1,0:T(8,128)}, f32[576,128]{1,0:T(8,128)S(1)}, u32[]{:S(2)}, u32[]{:S(2)}) collective-permute-start(f32[576,128]{1,0:T(8,128)} %get-tuple-element.21), channel_id=1, source_target_pairs={{0,96},{32,64},{64,32},{96,0},{1,97},{33,65},{65,33},{97,1},{2,98}... | collective-permute-start | bytes 884744 | tf_op jit(solution)/shard_map/ppermute | solution.py:301
  93.0 0.7 copy-start.7
  93.0 0.8 copy-start.8
  105.6 3.8 %collective-permute-start.6 = (f32[256,128]{1,0:T(8,128)}, f32[256,128]{1,0:T(8,128)S(1)}, u32[]{:S(2)}, u32[]{:S(2)}) collective-permute-start(f32[256,128]{1,0:T(8,128)} %get-tuple-element.24.own_g), channel_id=1, source_target_pairs={{0,1},{1,0},{2,3},{3,2},{4,5},{5,4},{6,7},{7,6},{8,9},{9,8},{10,11... | collective-permute-start | bytes 393224 | tf_op jit(solution)/shard_map/ppermute | solution.py:302
  107.6 12.5 %collective-permute-start.7 = (f32[256,128]{1,0:T(8,128)}, f32[256,128]{1,0:T(8,128)S(1)}, u32[]{:S(2)}, u32[]{:S(2)}) collective-permute-start(f32[256,128]{1,0:T(8,128)} %get-tuple-element.24.own_g), channel_id=1, source_target_pairs={{0,31},{1,2},{2,1},{3,4},{4,3},{5,6},{6,5},{7,8},{8,7},{9,10},{10,... | collective-permute-start | bytes 393224 | tf_op jit(solution)/shard_map/ppermute | solution.py:301
  120.1 13.7 %copy-start.3 = (f32[768,128]{1,0:T(8,128)}, f32[768,128]{1,0:T(8,128)S(1)}, u32[]{:S(2)}) copy-start(f32[768,128]{1,0:T(8,128)S(1)} %constant_dynamic-update-slice_fusion.middle.g1) | copy-start | bytes 1179652
  120.1 9.8 %collective-permute-start.9 = (f32[768,128]{1,0:T(8,128)S(1)}, f32[768,128]{1,0:T(8,128)S(1)}, u32[]{:S(2)}, u32[]{:S(2)}) collective-permute-start(f32[768,128]{1,0:T(8,128)S(1)} %constant_dynamic-update-slice_fusion.middle.g1), channel_id=1, source_target_pairs={{0,384},{128,256},{256,128},{384,0},{1,385},{129,257},{257,129},{3... | collective-permute-start | bytes 1179656 | tf_op jit(solution)/shard_map/ppermute | solution.py:301
  124.1 9.7 %collective-permute-start.8 = (f32[768,128]{1,0:T(8,128)S(1)}, f32[768,128]{1,0:T(8,128)S(1)}, u32[]{:S(2)}, u32[]{:S(2)}) collective-permute-start(f32[768,128]{1,0:T(8,128)S(1)} %constant_dynamic-update-slice_fusion.middle.g1), channel_id=1, source_target_pairs={{0,128},{128,0},{256,384},{384,256},{1,129},{129,1},{257,385},{385... | collective-permute-start | bytes 1179656 | tf_op jit(solution)/shard_map/ppermute | solution.py:302
  129.9 3.9 %copy-start.4 = (f32[768,128]{1,0:T(8,128)}, f32[768,128]{1,0:T(8,128)S(1)}, u32[]{:S(2)}) copy-start(f32[768,128]{1,0:T(8,128)S(1)} %collective-permute-done.9.other_side.g2) | copy-start | bytes 1179652
  133.8 0.7 copy-start.5
  137.4 8.8 %collective-permute-start.10 = (f32[576,128]{1,0:T(8,128)}, f32[576,128]{1,0:T(8,128)S(1)}, u32[]{:S(2)}, u32[]{:S(2)}) collective-permute-start(f32[576,128]{1,0:T(8,128)} %get-tuple-element.25), channel_id=1, source_target_pairs={{0,32},{32,0},{64,96},{96,64},{1,33},{33,1},{65,97},{97,65},{2,34}... | collective-permute-start | bytes 884744 | tf_op jit(solution)/shard_map/ppermute | solution.py:302
  140.8 12.0 %collective-permute-start.11 = (f32[576,128]{1,0:T(8,128)}, f32[576,128]{1,0:T(8,128)S(1)}, u32[]{:S(2)}, u32[]{:S(2)}) collective-permute-start(f32[576,128]{1,0:T(8,128)} %get-tuple-element.26), channel_id=1, source_target_pairs={{0,96},{32,64},{64,32},{96,0},{1,97},{33,65},{65,33},{97,1},{2,98}... | collective-permute-start | bytes 884744 | tf_op jit(solution)/shard_map/ppermute | solution.py:301
  146.2 6.5 %copy-start.9 = (f32[576,128]{1,0:T(8,128)}, f32[576,128]{1,0:T(8,128)S(1)}, u32[]{:S(2)}) copy-start(f32[576,128]{1,0:T(8,128)S(1)} %collective-permute-done.10.g3) | copy-start | bytes 884740
  152.8 0.7 copy-start.10

commit v2 on v1

--- a/solution.py
+++ b/solution.py
@@ -44,20 +44,51 @@
     return SHELL.index(tuple(-step for step in offset)), False
 
 
-def pair_rows():
-    rows = [(SLOTS[0], SLOTS[0], 0, True), (SLOTS[0], SLOTS[0], 0, False)]
-    rows += [(SLOTS[0], o, *shell_place(o)) for o in AROUND]
-    for side in (1, -1):
-        for sx in (-1, 0, 1):
-            for sz in (-1, 0, 1):
-                rows.append(((0, -side, 0), (sx, side, sz), *shell_place((sx, side, sz))))
-    picked = np.zeros((len(rows), 28 * 14), np.float32)
-    forward = np.zeros((len(rows), 1), bool)
-    for i, (reader, offset, index_k, ahead) in enumerate(rows):
+SLOT_ROWS = 32
+LIST_ROWS = 56
+SENT = [(sx, sz) for sx in (-1, 0, 1) for sz in (-1, 0, 1)]
+
+
+def list_selectors(sides):
+    rows = {0: (SLOTS[0], SLOTS[0], 0, True), 1: (SLOTS[0], SLOTS[0], 0, False)}
+    for i, offset in enumerate(AROUND):
+        rows[2 + i] = (SLOTS[0], offset, *shell_place(offset))
+    for j, side in enumerate(sides):
+        for m, (sx, sz) in enumerate(SENT):
+            offset = (sx, side, sz)
+            rows[SLOT_ROWS + 9 * j + m] = ((0, -side, 0), offset, *shell_place(offset))
+    holders = np.zeros((LIST_ROWS, SLOT_ROWS), np.float32)
+    lanes = np.zeros((4, LIST_ROWS, 128), np.float32)
+    for i, (reader, offset, index_k, ahead) in rows.items():
         holder = reader if ahead else tuple(a + b for a, b in zip(reader, offset))
-        picked[i, SLOTS.index(holder) * 14 + index_k] = 1.0
-        forward[i, 0] = ahead
-    return picked, forward
+        holders[i, SLOTS.index(holder)] = 1.0
+        for q in range(4):
+            lanes[q, i, 1 + 4 * index_k + (q if ahead else (q + 2) % 4)] = 1.0
+    return holders, lanes
+
+
+def list_bases():
+    def place_of(steps, odd):
+        return 1 - steps * (1 - 2 * odd)
+
+    def rows(odd_x, odd_y, odd_z):
+        bases = np.zeros((LIST_ROWS, 3), np.float32)
+        for i, (sx, sy, sz) in enumerate(SLOTS):
+            if sy == 0:
+                first = (place_of(sx, odd_x) * 3 + place_of(sz, odd_z)) * 256
+                bases[i] = first, first, TILE
+            else:
+                listed = (sx + 1) * 3 + sz + 1
+                first = NINE + 576 * place_of(sy, odd_y) // 2 + listed * 2 * TILE
+                bases[i] = first, first + TILE, 0
+        for i, (sx, sz) in enumerate(SENT):
+            first = (place_of(sx, odd_x) * 3 + place_of(sz, odd_z)) * 256
+            for at in (SLOT_ROWS + i, SLOT_ROWS + 9 + i):
+                bases[at] = first, first, TILE
+        return bases
+
+    even = rows(0, 0, 0)
+    return np.stack([even, rows(1, 0, 0) - even, rows(0, 1, 0) - even, rows(0, 0, 1) - even])
 
 
 def whole(array):
@@ -74,16 +105,156 @@
 NINE = 9 * 256
 AROUND_ROWS = NINE + 2 * 18 * TILE
 BODIES = SLABS // BODY
+WIDE = 2 * SLOT_ROWS * TILE
+IDLE = 28 * TILE
 STEP = 2
 STEPS = BODIES // STEP
 
 
+def prepare_kernel(
+    where, everyone, holders, lanes, bases, side, shift, own_side, units,
+    table, order, own_rows, other_rows, lists, count, at_unit
+):
+    f32 = jnp.float32
+    odd = [where[a] & 1 for a in range(3)]
+    device = ((where[0] + side[:, 0:1]) & 3) * 4 + ((where[1] + side[:, 1:2]) & 3)
+    device = device * 3 + 1 - side[:, 2:3] * (1 - 2 * odd[2])
+    device = jnp.where(side[:, 3:4] > 0, device, -1)
+    devices = lax.broadcasted_iota(jnp.int32, (SLOT_ROWS, 48), 1)
+    slots = exact_dot(jnp.where(devices == device, 1.0, 0.0), everyone[...])
+    numbers = slots[:, 768:896]
+    rows = exact_dot(holders[odd[1]], numbers)
+    tiles = [jnp.sum(rows * lanes[odd[1], q], axis=1, keepdims=True) for q in range(4)]
+    lane = lax.broadcasted_iota(jnp.int32, (LIST_ROWS, 128), 1)
+    base = bases[0]
+    for a in range(3):
+        base = base + bases[1 + a] * odd[a].astype(f32)
+    place = [base[:, n : n + 1] + base[:, 2:3] * tiles[2 + n] for n in range(2)]
+    listed = jnp.where(lane < 1, tiles[0], jnp.where(lane < 2, tiles[1], place[1]))
+    listed = jnp.where(lane == 2, place[0], listed)
+    lists[...] = jnp.round(listed).astype(jnp.int32)
+
+    slot = lax.broadcasted_iota(jnp.int32, (SLOT_ROWS, 1), 0)
+    halves = []
+    for n in range(2):
+        own = tiles[n][0:SLOT_ROWS]
+        other = tiles[2 + n][0:SLOT_ROWS]
+        at = []
+        for c in range(3):
+            acc = jnp.zeros((SLOT_ROWS, TILE), f32)
+            for t in range(8):
+                first = c * 256 + t * TILE
+                acc = acc + jnp.where(jnp.abs(other - t) < 0.5, slots[:, first : first + TILE], 0.0)
+            at.append(acc + shift[:, c : c + 1])
+        same = jnp.where((jnp.abs(own - other) < 0.5) & (slot < 2), 1.0, 0.0)
+        own_left = numbers[0:1, 0:1] - own * TILE
+        other_left = numbers[:, 0:1] - other * TILE
+        rest = jnp.where(lane[0:SLOT_ROWS, 0:TILE] == 0, own, 0.0)
+        for q, value in enumerate((own_left, other_left, same, place[n][0:SLOT_ROWS] * (1.0 / TILE))):
+            rest = jnp.where(lane[0:SLOT_ROWS, 0:TILE] == q + 1, value, rest)
+        halves.append(jnp.concatenate([*at, rest], axis=1))
+    per_unit = jnp.concatenate(halves, axis=0)
+    at_unit[...] = per_unit
+    per_slab = jnp.dot(in_thirds(per_unit.T), units[...], preferred_element_type=f32)
+
+    slab = lax.broadcasted_iota(jnp.int32, (TILE, WIDE), 1)
+    u = lax.broadcasted_iota(jnp.int32, (TILE, WIDE), 0)
+    w = slab & (TILE - 1)
+    own_tile = per_slab[96:97]
+    eight = lax.broadcasted_iota(jnp.int32, (8, WIDE), 0).astype(f32)
+    chosen = jnp.where(jnp.abs(own_tile - eight) < 0.5, 1.0, 0.0).astype(jnp.bfloat16)
+    own_at = jnp.dot(
+        in_thirds(own_side[...]), jnp.concatenate([chosen] * 3, axis=0), preferred_element_type=f32
+    )
+    square = jnp.full((TILE, WIDE), SOFTEN * SOFTEN, f32)
+    for c in range(3):
+        part = slice(c * TILE, (c + 1) * TILE)
+        other_at = jnp.sum(jnp.where(u == w, per_slab[part], 0.0), axis=0, keepdims=True)
+        sep = other_at - own_at[part]
+        square = square + sep * sep
+    dist = jnp.sqrt(square)
+    reverse = ((slab >> 5) & (SLOT_ROWS - 1)) == 1
+    away = jnp.where(reverse, u - w, w - u)
+    drop = (per_slab[99:100] > 0.5) & (away <= 0)
+    fits = (u.astype(f32) < per_slab[97:98]) & (w.astype(f32) < per_slab[98:99])
+    usable = fits & (dist < 1.0) & jnp.logical_not(drop)
+    angle = math.pi * dist
+    near = 1.0 / dist
+    cut = jnp.where(usable, 0.5 * (jnp.cos(angle) + 1.0), 0.0)
+    table[0:TILE, :] = KAPPA * dist
+    table[TILE : 2 * TILE, :] = cut
+    table[2 * TILE : 3 * TILE, :] = cut * (-2.0 * GAMMA / KAPPA) * near
+    table[3 * TILE : 4 * TILE, :] = jnp.where(usable, -0.5 * math.pi * jnp.sin(angle), 0.0) * near
+
+    live = jnp.max(jnp.where(usable, 1.0, 0.0), axis=0, keepdims=True)
+    blocks = WIDE // 128
+    live = jnp.concatenate([live[:, b * 128 : (b + 1) * 128] for b in range(blocks)], axis=0)
+    row = lax.broadcasted_iota(jnp.int32, (128, 128), 0)
+    col = lax.broadcasted_iota(jnp.int32, (128, 128), 1)
+    upto = jnp.where(row <= col, 1.0, 0.0).astype(jnp.bfloat16)
+    until = jnp.dot(live.astype(jnp.bfloat16), upto, preferred_element_type=f32)
+    sums = jnp.broadcast_to(until[:, 127:128], (blocks, 128)).astype(jnp.bfloat16)
+    below = jnp.where(row > col, 1.0, 0.0).astype(jnp.bfloat16)[0:blocks, 0:blocks]
+    before = jnp.dot(below, sums, preferred_element_type=f32)
+    rank = jnp.where(live > 0.5, until + before - 1.0, -1.0)
+    total = before[blocks - 1 : blocks, :] + until[blocks - 1 : blocks, 127:128]
+    bodies = jnp.floor((total + (BODY - 1.0)) * (1.0 / BODY))
+    count[...] = jnp.broadcast_to(bodies, (8, 128)).astype(jnp.int32)
+    target = lax.broadcasted_iota(jnp.int32, (SLABS, 256), 0).astype(f32)
+    names_row = lax.broadcasted_iota(jnp.int32, (8, 256), 0)
+    names_lane = lax.broadcasted_iota(jnp.int32, (8, 256), 1)
+    found = jnp.zeros((8, SLABS), f32)
+    for b in range(blocks // 2):
+        wide_rank = jnp.concatenate([rank[2 * b : 2 * b + 1], rank[2 * b + 1 : 2 * b + 2]], axis=1)
+        hit = jnp.where(target == wide_rank, 1.0, 0.0).astype(jnp.bfloat16)
+        names = jnp.where(names_row == 0, b * 8 + (names_lane >> 5), names_lane & (TILE - 1))
+        names = jnp.where(names_row == 2, 1, names).astype(f32)
+        part = slice(b * 256, (b + 1) * 256)
+        names = jnp.where(names_row == 3, per_slab[96:97, part], names)
+        names = jnp.where(names_row == 4, per_slab[100:101, part], names)
+        found = found + nt_dot(names.astype(jnp.bfloat16), hit)
+    named = jnp.where(found[2:3] > 0.5, found[0:1] * TILE + found[1:2], 1.0 * IDLE)
+    order[...] = jnp.round(named).astype(jnp.int32)
+    own_rows[...] = jnp.round(found[3:4] * TILE).astype(jnp.int32)
+    other_rows[...] = jnp.round(found[4:5] * TILE + found[1:2]).astype(jnp.int32)
+
+
+def in_thirds(values):
+    high = values.astype(jnp.bfloat16)
+    rest = values - high.astype(jnp.float32)
+    middle = rest.astype(jnp.bfloat16)
+    low = (rest - middle.astype(jnp.float32)).astype(jnp.bfloat16)
+    return jnp.concatenate([high, middle, low], axis=1)
+
+
+def prepare(where, *arrays):
+    outs = [
+        jax.ShapeDtypeStruct((128, WIDE), jnp.float32),
+        *[jax.ShapeDtypeStruct((1, SLABS), jnp.int32)] * 3,
+        jax.ShapeDtypeStruct((LIST_ROWS, 128), jnp.int32),
+        jax.ShapeDtypeStruct((8, 128), jnp.int32),
+        jax.ShapeDtypeStruct((2 * SLOT_ROWS, 128), jnp.float32),
+    ]
+    return pl.pallas_call(
+        prepare_kernel,
+        grid_spec=pltpu.PrefetchScalarGridSpec(
+            num_scalar_prefetch=1,
+            grid=(1,),
+            in_specs=[whole(a) for a in arrays],
+            out_specs=[whole(o) for o in outs],
+        ),
+        out_shape=outs,
+        compiler_params=pltpu.CompilerParams(vmem_limit_bytes=VMEM),
+        name="distances_and_live_rows",
+    )(where, *arrays)
+
+
 def last_block(step, count):
-    return jnp.minimum(step, jnp.maximum((count[0] + STEP - 1) // STEP - 1, 0))
+    return jnp.minimum(step, jnp.maximum((count[0, 0] + STEP - 1) // STEP - 1, 0))
 
 
 def bodies_of(step, count):
-    return jnp.clip(count[0] - step * STEP, 0, STEP)
+    return jnp.clip(count[0, 0] - step * STEP, 0, STEP)
 
 
 def filter_kernel(count, order, table, centres, first_w, second_w, first_b, second_b, out, out_d):
@@ -92,9 +263,9 @@
     def one(index, carry):
         spread = [[], [], [], []]
         for j in range(BODY):
-            slab = order[(step * STEP + index) * BODY + j]
-            lanes = pl.ds(pl.multiple_of(slab // 128 * 128, 128), 128)
-            lane = jnp.full((TILE, 128), slab % 128, jnp.int32)
+            slab = order[0, (step * STEP + index) * BODY + j]
+            lanes = pl.ds(pl.multiple_of((slab >> 7) << 7, 128), 128)
+            lane = jnp.full((TILE, 128), slab & 127, jnp.int32)
             for q in range(4):
                 values = table[q * TILE : (q + 1) * TILE, lanes]
                 spread[q].append(jnp.take_along_axis(values, lane, axis=1, mode="promise_in_bounds"))
@@ -145,12 +316,12 @@
         row += piece.shape[0]
 
 
-def gather_kernel(starts, one_side, middle, other_side, near, far, held):
+def gather_kernel(lists, one_side, middle, other_side, near, far, held):
     laid_end_to_end((one_side, middle, other_side), held)
 
     def one(index, carry):
-        a = pl.multiple_of(starts[index], TILE)
-        b = pl.multiple_of(starts[18 + index], TILE)
+        a = pl.multiple_of(lists[SLOT_ROWS + (index >> 1), 2 + (index & 1)], TILE)
+        b = pl.multiple_of(lists[SLOT_ROWS + 9 + (index >> 1), 2 + (index & 1)], TILE)
         o = pl.multiple_of(index * TILE, TILE)
         near[pl.ds(o, TILE), :] = held[pl.ds(a, TILE), :]
         far[pl.ds(o, TILE), :] = held[pl.ds(b, TILE), :]
@@ -159,7 +330,7 @@
     lax.fori_loop(0, 18, one, 0)
 
 
-def gather_tiles(starts, pieces):
+def gather_tiles(lists, pieces):
     shape = (18 * TILE, 128)
     outs = [jax.ShapeDtypeStruct(shape, jnp.float32)] * 2
     return pl.pallas_call(
@@ -174,7 +345,7 @@
         out_shape=outs,
         compiler_params=pltpu.CompilerParams(vmem_limit_bytes=VMEM),
         name="tiles_to_send",
-    )(starts, *pieces)
+    )(lists, *pieces)
 
 
 def softplus(values):
@@ -189,7 +360,7 @@
 
 
 def message_kernel(
-    count, order, tiles, starts, filt, p0, p1, p2, p3, p4, feats, cot, out_w, out_b, fin_w, fin_b,
+    count, order, own_rows, other_rows, filt, p0, p1, p2, p3, p4, feats, cot, out_w, out_b, fin_w, fin_b,
     new, grad, near, *totals
 ):
     step = pl.program_id(0)
@@ -202,11 +373,10 @@
 
     def one(index, carry):
         for j in range(BODY):
-            slab = order[(step * STEP + index) * BODY + j]
-            unit = slab // TILE
-            h = near[pl.ds(starts[unit] + slab % TILE, 1), :]
+            at = (step * STEP + index) * BODY + j
+            h = near[pl.ds(other_rows[0, at], 1), :]
             rows = pl.ds(pl.multiple_of(index * ROWS + j * TILE, TILE), TILE)
-            own = pl.ds(pl.multiple_of(tiles[unit] * TILE, TILE), TILE)
+            own = pl.ds(pl.multiple_of(own_rows[0, at], TILE), TILE)
             total = totals[j % CHAINS]
             total[own, :] = total[own, :] + filt[rows, :].astype(jnp.float32) * h
         return carry
@@ -226,7 +396,7 @@
 
 
 def back_kernel(
-    count, order, tiles, starts, filt, filt_d, h0, h1, h2, h3, h4, g0, g1, g2, g3, g4, own_h, own_g,
+    count, order, own_rows, other_rows, filt, filt_d, h0, h1, h2, h3, h4, g0, g1, g2, g3, g4, own_h, own_g,
     r_near, r_own, cot, in_w, grad, force, near, g_near, *totals
 ):
     step = pl.program_id(0)
@@ -244,13 +414,13 @@
         slopes = []
         places = []
         for j in range(BODY):
-            slab = order[(step * STEP + index) * BODY + j]
-            unit = slab // TILE
-            row = pl.ds(starts[unit] + slab % TILE, 1)
+            at = (step * STEP + index) * BODY + j
+            slab = order[0, at]
+            row = pl.ds(other_rows[0, at], 1)
             h = near[row, :]
             g = g_near[row, :]
             rows = pl.ds(pl.multiple_of(index * ROWS + j * TILE, TILE), TILE)
-            own = pl.ds(pl.multiple_of(tiles[unit] * TILE, TILE), TILE)
+            own = pl.ds(pl.multiple_of(own_rows[0, at], TILE), TILE)
             total = totals[j % CHAINS]
             total[own, :] = total[own, :] + filt[rows, :].astype(jnp.float32) * g
             mixed = filt_d[rows, :].astype(jnp.float32) * (own_g[own, :] * h + own_h[own, :] * g)
@@ -300,10 +470,6 @@
     far = [(i, ((i ^ 1) + 2 * (2 * (i % 2) - 1)) % size) for i in range(size)]
     from_far = lax.ppermute(to_far, axis, far)
     return lax.ppermute(to_near, axis, near), from_far
-
-
-def place_of(steps, axis):
-    return 1 - steps * (1 - 2 * (lax.axis_index(axis) % 2))
 
 
 def planes(own):
@@ -361,80 +527,25 @@
     ).reshape(along * across, 24 * 128)
     everyone = everyone.reshape(along * across * 3, 8 * 128)
     side = np.array(SLOTS)
-    holders = (lax.axis_index("gx") + side[:, 0]) % along * across
-    holders = (holders + (lax.axis_index("gy") + side[:, 1]) % across) * 3
-    holders = holders + place_of(side[:, 2], "gz")
-    picker = (holders[:, None] == jnp.arange(along * across * 3)[None, :]).astype(jnp.float32)
-    slots = exact_dot(picker, everyone)
-
-    picked, forward = pair_rows()
-    lists = exact_dot(picked, slots[:, 769:825].reshape(28 * 14, 4))
-    lists = jnp.round(lists).astype(jnp.int32)
-    mine = jnp.where(forward, lists[:, 0:2], lists[:, 2:4])
-    theirs = jnp.where(forward, lists[:, 2:4], lists[:, 0:2])
-    own_tiles, other_tiles = mine[:28], theirs[:28]
-    column = (place_of(side[:, 0], "gx") * 3 + place_of(side[:, 2], "gz"))[:, None]
-    listed = ((side[:, 0] + 1) * 3 + side[:, 2] + 1)[:, None]
-    entry = np.arange(2)[None]
-    starts = jnp.where(
-        (side[:, 1] == 0)[:, None],
-        column * 256 + other_tiles * TILE,
-        NINE + 288 * place_of(side[:, 1:2], "gy") + (listed * 2 + entry) * TILE,
-    )
-    sent = np.array([(sx, sz) for sx in (-1, 0, 1) for sz in (-1, 0, 1)])
-    sent_column = (place_of(sent[:, 0], "gx") * 3 + place_of(sent[:, 1], "gz"))[:, None]
-    wanted = sent_column * 256 + theirs[28:].reshape(2, 9, 2) * TILE
-    lower, upper = wanted[0].reshape(18), wanted[1].reshape(18)
-    even = lax.axis_index("gy") % 2 == 0
-    wanted = jnp.concatenate([jnp.where(even, upper, lower), jnp.where(even, lower, upper)])
-
-    pick_other = (other_tiles[:, :, None] == jnp.arange(8)).astype(jnp.float32)
-    slot_pos = slots[:, : 6 * 128].reshape(28, 1, 3, 8, TILE)
-    shift = np.repeat(np.array(SLOTS, np.float32), 2, axis=0)
-    other_at = jnp.sum(pick_other[:, :, None, :, None] * slot_pos, axis=3).reshape(UNITS, 3, TILE)
-    other_at = other_at + shift[:, :, None]
-    same = ((own_tiles == other_tiles) & (np.arange(28) < 2)[:, None]).astype(jnp.float32)
-    per_unit = jnp.stack(
-        [
-            own_tiles.astype(jnp.float32),
-            slots[0:1, 768:769] - own_tiles * TILE,
-            slots[:, 768:769] - other_tiles * TILE,
-            same,
-        ]
-    ).reshape(4, UNITS)
-    slab = np.arange(SLABS)
-    per_slab = exact_dot(per_unit, (slab[None] // TILE == np.arange(UNITS)[:, None]).astype(np.float32))
-    own_side = own_pos.reshape(3, 8, TILE).transpose(0, 2, 1).reshape(96, 8)
-    own_at = exact_dot(
-        own_side, (per_slab[0:1] == np.arange(8, dtype=np.float32)[:, None]).astype(jnp.float32)
-    ).reshape(3, TILE, SLABS)
-    other_row = other_at.transpose(1, 0, 2).reshape(3, 1, SLABS)
-    sep = other_row - own_at
-    dist = jnp.sqrt(sep[0] * sep[0] + sep[1] * sep[1] + sep[2] * sep[2] + SOFTEN * SOFTEN)
-    w = jnp.asarray(slab % TILE, jnp.float32)[None]
-    u = jnp.asarray(np.arange(TILE), jnp.float32)[:, None]
-    reverse = jnp.asarray(slab // TILE >= 2)[None]
-    drop = (per_slab[3:4] > 0.5) & jnp.where(reverse, w >= u, u >= w)
-    usable = (u < per_slab[1:2]) & (w < per_slab[2:3]) & (dist < 1.0) & ~drop
-    angle = math.pi * dist
-    cut = jnp.where(usable, 0.5 * (jnp.cos(angle) + 1.0), 0.0)
-    gain = cut * (-2.0 * GAMMA / KAPPA) / dist
-    slope = jnp.where(usable, -0.5 * math.pi * jnp.sin(angle), 0.0) / dist
-    table = jnp.pad(
-        jnp.concatenate([KAPPA * dist, cut, gain, slope], axis=0), ((0, 0), (0, 128))
-    )
-    live = jnp.max(usable.astype(jnp.float32), axis=0).reshape(SLABS // 128, 128)
-    until = exact_dot(live, np.triu(np.ones((128, 128), np.float32)))
-    before = exact_dot(np.tril(np.ones((14, 14), np.float32), -1), until[:, 127:128])
-    rank = jnp.where(live > 0.5, until + before - 1.0, -1.0).reshape(1, SLABS)
-    total = jnp.sum(live).astype(jnp.int32)
-    hit = rank == jnp.asarray(slab, jnp.float32)[:, None]
-    order = jnp.sum(jnp.where(hit, jnp.asarray(slab)[None], 0), axis=1)
-    order = jnp.where(slab < total, order, SLABS).astype(jnp.int32)
-    count = ((total + BODY - 1) // BODY).reshape(1)
-
+    sides = np.zeros((SLOT_ROWS, 4), np.int32)
+    sides[:28, :3] = side
+    sides[:28, 3] = 1
+    selectors = [list_selectors((-1, 1)), list_selectors((1, -1))]
+    units = np.arange(WIDE)[None] // TILE == np.arange(2 * SLOT_ROWS)[:, None]
+    where = jnp.stack([lax.axis_index(axis) for axis in ("gx", "gy", "gz")]).astype(jnp.int32)
+    table, order, own_rows, other_rows, lists, count, at_unit = prepare(
+        where,
+        everyone,
+        jnp.asarray(np.stack([rows for rows, _ in selectors])),
+        jnp.asarray(np.stack([lanes for _, lanes in selectors])),
+        jnp.asarray(list_bases()),
+        jnp.asarray(sides),
+        jnp.asarray(sides[:, :3].astype(np.float32)),
+        own_pos.reshape(3, 8, TILE).transpose(0, 2, 1).reshape(96, 8),
+        jnp.asarray(np.tile(units, (3, 1)).astype(jnp.bfloat16)),
+    )
     near_x = columns(hidden_three)
-    to_near, to_far, count = lax.optimization_barrier((*gather_tiles(wanted, near_x), count))
+    to_near, to_far, count = lax.optimization_barrier((*gather_tiles(lists, near_x), count))
     near = [*near_x, *swapped(to_far, to_near, "gy")]
     filt, filt_d = filters(
         count,
@@ -446,12 +557,7 @@
         filter_bias[None],
     )
     cot = cotangent.reshape(256, 128)
-    scalars = (
-        count,
-        order,
-        jnp.pad(own_tiles.reshape(UNITS), (0, 8)),
-        jnp.pad(starts.reshape(UNITS), (0, 8)).astype(jnp.int32),
-    )
+    scalars = (count, order, own_rows, other_rows)
     new_features, d_msg = pair_call(
         message_kernel,
         scalars,
@@ -474,9 +580,10 @@
         "messages_and_update",
     )
     g_x = columns(planes(d_msg))
-    to_near, to_far = gather_tiles(wanted, g_x)
+    to_near, to_far = gather_tiles(lists, g_x)
     g_near = [*g_x, *swapped(to_far, to_near, "gy")]
-    r_near = jnp.pad(other_at.transpose(0, 2, 1).reshape(SLABS, 3), ((0, 8), (0, 125)))
+    r_near = at_unit[:, :96].reshape(2 * SLOT_ROWS, 3, TILE).transpose(0, 2, 1).reshape(WIDE, 3)
+    r_near = jnp.pad(r_near, ((0, 0), (0, 125)))
     r_own = jnp.pad(own_pos.T, ((0, 0), (0, 125)))
     grad_features, force = pair_call(
         back_kernel,

time: 174 us -> 162 us (0.931)
  the two profiles are of different devices: /device:TPU:12 before, /device:TPU:10 now
where the time goes in v2:
time: 162 us; the launch traced here: 160 us
  Pallas kernels  63.8 us (39%)
  starting transfers between devices  51 us (31%)
  waiting for transfers between devices  28.2 us (17%)
  local copies, waits for them, and re-layouts  11.5 us (7%)
  other arithmetic  3.07 us (2%)
    ppermute x6, starting transfers between devices, swapped(): from_far = lax.ppermute(to_far, axis, far)  30.3 us
    pallas_call x2, Pallas kernels, pair_call(): pl.pallas_call(body, grid_spec=pltpu.PrefetchScalarGridSpec(num_scalar_pr...  24.7 us
    pallas_call x1, Pallas kernels, filters(): pl.pallas_call(filter_kernel, grid_spec=pltpu.PrefetchScalarGridSpec(num_...  24.3 us
    ppermute x6, waiting for transfers between devices, swapped(): from_far = lax.ppermute(to_far, axis, far)  19.7 us
    ppermute x6, starting transfers between devices, swapped(): return (lax.ppermute(to_near, axis, near), from_far)  15.3 us
    pallas_call x1, Pallas kernels, prepare(): pl.pallas_call(prepare_kernel, grid_spec=pltpu.PrefetchScalarGridSpec(num...  7.96 us
    pallas_call x2, Pallas kernels, gather_tiles(): pl.pallas_call(gather_kernel, grid_spec=pltpu.PrefetchScalarGridSpec(num_...  6.88 us
    unnamed x31, local copies, waits for them, and re-layouts  5.61 us
  transfers between devices with their start and end apart: 13, of which 7 were waited for; matrix products, arithmetic and copies ran while one was open for 5% of the time, Pallas kernels for 20%

profile of v2, /device:TPU:10, one launch (start us, length us, event | category | flops | bytes accessed | tf_op | source)
XLA Modules:
  0.0 160.2 jit_solution(17647424500657424264)
XLA Ops:
  2.0 0.8 copy.29
  3.1 1.0 fusion.6.own_h
  4.2 14.7 %collective-permute-start.1 = (f32[1,264,128]{2,1,0:T(8,128)S(1)}, f32[1,264,128]{2,1,0:T(8,128)S(1)}, u32[]{:S(2)}, u32[]{:S(2)}) collective-permute-start(f32[1,264,128]{2,1,0:T(8,128)S(1)} %maximum_bitcast_fusion), channel_id=1, source_target_pairs={{0,31},{1,2},{2,1},{3,4},{4,3},{5,6},{6,5},{7,8},{8,7},{9,10},{10,... | collective-permute-start | bytes 405512 | tf_op jit(solution)/shard_map/ppermute | solution.py:471
  18.9 1.9 %collective-permute-start = (f32[1,264,128]{2,1,0:T(8,128)S(1)}, f32[1,264,128]{2,1,0:T(8,128)S(1)}, u32[]{:S(2)}, u32[]{:S(2)}) collective-permute-start(f32[1,264,128]{2,1,0:T(8,128)S(1)} %maximum_bitcast_fusion), channel_id=1, source_target_pairs={{0,1},{1,0},{2,3},{3,2},{4,5},{5,4},{6,7},{7,6},{8,9},{9,8},{10,11... | collective-permute-start | bytes 405512 | tf_op jit(solution)/shard_map/ppermute | solution.py:472
  20.9 1.1 collective-permute-done.1
  22.2 3.4 %collective-permute-start.3 = (f32[768,128]{1,0:T(8,128)S(1)}, f32[768,128]{1,0:T(8,128)S(1)}, u32[]{:S(2)}, u32[]{:S(2)}) collective-permute-start(f32[768,128]{1,0:T(8,128)S(1)} %bitcast.37), channel_id=1, source_target_pairs={{0,384},{128,256},{256,128},{384,0},{1,385},{129,257},{257,129},{3... | collective-permute-start | bytes 1179656 | tf_op jit(solution)/shard_map/ppermute | solution.py:471
  25.6 3.7 %collective-permute-start.2 = (f32[768,128]{1,0:T(8,128)S(1)}, f32[768,128]{1,0:T(8,128)S(1)}, u32[]{:S(2)}, u32[]{:S(2)}) collective-permute-start(f32[768,128]{1,0:T(8,128)S(1)} %bitcast.38), channel_id=1, source_target_pairs={{0,128},{128,0},{256,384},{384,256},{1,129},{129,1},{257,385},{385... | collective-permute-start | bytes 1179656 | tf_op jit(solution)/shard_map/ppermute | solution.py:472
  30.0 5.3 %all-to-all-start = ((f32[16,24,128]{2,1,0:T(8,128)}), f32[16,24,128]{2,1,0:T(8,128)S(1)}, u32[]{:S(2)}, u32[]{:S(2)}) async-start(f32[16,24,128]{2,1,0:T(8,128)} %broadcast_in_dim.32), calls=%async_computation | async-start | bytes 393216 | tf_op jit(solution)/shard_map/all_to_all | solution.py:522
  36.8 4.4 %all-to-all-done = f32[16,24,128]{2,1,0:T(8,128)S(1)} async-done(((f32[16,24,128]{2,1,0:T(8,128)}), f32[16,24,128]{2,1,0:T(8,128)S(1)}, u32[]{:S(2)}, u32[]{:S(2)}) %all-to-all-start) | async-done | bytes 196640 | tf_op jit(solution)/shard_map/all_to_all | solution.py:522
  41.9 8.0 %distances_and_live_rows.1 = (f32[128,2048]{1,0:T(8,128)}, s32[1,1792]{1,0:T(1,128)}, s32[1,1792]{1,0:T(1,128)}, s32[1,1792]{1,0:T(1,128)}, s32[56,128]{1,0:T(8,...) custom-call(s32[3]{0:T(128)} %pad_add_fusion.where, f32[48,1024]{1,0:T(8,128)} %reshape_reshape.11.everyone, ...), custom_call_target="tpu_custom_call" | custom-call | tf_op jit(solution)/shard_map/distances_and_live_rows/pallas_call | solution.py:238
  50.8 3.5 %tiles_to_send.2 = (f32[576,128]{1,0:T(8,128)}, f32[576,128]{1,0:T(8,128)}) custom-call(s32[56,128]{1,0:T(8,128)} %get-tuple-element.23.lists, f32[768,128]{1,0:T(8,128)} %copy-done.2, f32[768,128]{1,0:T(8,128)} %bitcast.39, f32[768,128]{1,0:T(8,128)} %copy-done.1), custom_call_target="tpu_custom_call" | custom-call | tf_op jit(solution)/shard_map/tiles_to_send/pallas_call | solution.py:336
  54.2 3.9 %collective-permute-start.4 = (f32[576,128]{1,0:T(8,128)}, f32[576,128]{1,0:T(8,128)S(1)}, u32[]{:S(2)}, u32[]{:S(2)}) collective-permute-start(f32[576,128]{1,0:T(8,128)} %get-tuple-element.33), channel_id=1, source_target_pairs={{0,32},{32,0},{64,96},{96,64},{1,33},{33,1},{65,97},{97,65},{2,34}... | collective-permute-start | bytes 884744 | tf_op jit(solution)/shard_map/ppermute | solution.py:472
  58.2 2.1 %collective-permute-start.5 = (f32[576,128]{1,0:T(8,128)}, f32[576,128]{1,0:T(8,128)S(1)}, u32[]{:S(2)}, u32[]{:S(2)}) collective-permute-start(f32[576,128]{1,0:T(8,128)} %get-tuple-element.34), channel_id=1, source_target_pairs={{0,96},{32,64},{64,32},{96,0},{1,97},{33,65},{65,33},{97,1},{2,98}... | collective-permute-start | bytes 884744 | tf_op jit(solution)/shard_map/ppermute | solution.py:471
  60.2 1.5 fusion.4
  61.8 24.3 %pair_filters.1 = (bf16[57344,128]{1,0:T(8,128)(2,1)}, bf16[57344,128]{1,0:T(8,128)(2,1)}) custom-call(s32[8,128]{1,0:T(8,128)} %get-tuple-element.27.count, s32[1,1792]{1,0:T(1,128)} %get-tuple-element.28.order, f32[128,2048]{1,0:T(8,128)} %get-tuple-element.31.table, f32[1,128]{1,0:T(1,128)} %constant.39.clone.centres, ...), custom_call_target="tpu_custom_call" | custom-call | tf_op jit(solution)/shard_map/pair_filters/pallas_call | solution.py:298
  86.9 9.6 %messages_and_update.1 = (bf16[256,128]{1,0:T(8,128)(2,1)}, f32[256,128]{1,0:T(8,128)}) custom-call(s32[8,128]{1,0:T(8,128)} %get-tuple-element.27.count, s32[1,1792]{1,0:T(1,128)} %get-tuple-element.28.order, s32[1,1792]{1,0:T(1,128)} %get-tuple-element.29.own_rows, s32[1,1792]{1,0:T(1,128)} %get-tuple-element.30.other_rows, ...), custom_call_target="tpu_custom_call" | custom-call | tf_op jit(solution)/shard_map/messages_and_update/pallas_call | solution.py:451
  96.5 1.9 %collective-permute-start.6 = (f32[256,128]{1,0:T(8,128)}, f32[256,128]{1,0:T(8,128)S(1)}, u32[]{:S(2)}, u32[]{:S(2)}) collective-permute-start(f32[256,128]{1,0:T(8,128)} %get-tuple-element.37.own_g), channel_id=1, source_target_pairs={{0,1},{1,0},{2,3},{3,2},{4,5},{5,4},{6,7},{7,6},{8,9},{9,8},{10,11... | collective-permute-start | bytes 393224 | tf_op jit(solution)/shard_map/ppermute | solution.py:472
  98.4 1.9 %collective-permute-start.7 = (f32[256,128]{1,0:T(8,128)}, f32[256,128]{1,0:T(8,128)S(1)}, u32[]{:S(2)}, u32[]{:S(2)}) collective-permute-start(f32[256,128]{1,0:T(8,128)} %get-tuple-element.37.own_g), channel_id=1, source_target_pairs={{0,31},{1,2},{2,1},{3,4},{4,3},{5,6},{6,5},{7,8},{8,7},{9,10},{10,... | collective-permute-start | bytes 393224 | tf_op jit(solution)/shard_map/ppermute | solution.py:471
  100.4 0.9 constant_dynamic-update-slice_fusion.1
  101.3 9.6 %collective-permute-done.7 = f32[256,128]{1,0:T(8,128)S(1)} collective-permute-done((f32[256,128]{1,0:T(8,128)}, f32[256,128]{1,0:T(8,128)S(1)}, u32[]{:S(2)}, u32[]{:S(2)}) %collective-permute-start.7) | collective-permute-done | bytes 131104 | tf_op jit(solution)/shard_map/ppermute | solution.py:471
  111.0 3.8 %collective-permute-start.9 = (f32[768,128]{1,0:T(8,128)S(1)}, f32[768,128]{1,0:T(8,128)S(1)}, u32[]{:S(2)}, u32[]{:S(2)}) collective-permute-start(f32[768,128]{1,0:T(8,128)S(1)} %constant_dynamic-update-slice_fusion.middle.g1), channel_id=1, source_target_pairs={{0,384},{128,256},{256,128},{384,0},{1,385},{129,257},{257,129},{3... | collective-permute-start | bytes 1179656 | tf_op jit(solution)/shard_map/ppermute | solution.py:471
  114.7 1.9 %collective-permute-start.8 = (f32[768,128]{1,0:T(8,128)S(1)}, f32[768,128]{1,0:T(8,128)S(1)}, u32[]{:S(2)}, u32[]{:S(2)}) collective-permute-start(f32[768,128]{1,0:T(8,128)S(1)} %constant_dynamic-update-slice_fusion.middle.g1), channel_id=1, source_target_pairs={{0,128},{128,0},{256,384},{384,256},{1,129},{129,1},{257,385},{385... | collective-permute-start | bytes 1179656 | tf_op jit(solution)/shard_map/ppermute | solution.py:472
  116.7 4.0 %collective-permute-done.9.other_side.g2 = f32[768,128]{1,0:T(8,128)S(1)} collective-permute-done((f32[768,128]{1,0:T(8,128)S(1)}, f32[768,128]{1,0:T(8,128)S(1)}, u32[]{:S(2)}, u32[]{:S(2)}) %collective-permute-start.9) | collective-permute-done | bytes 393248 | tf_op jit(solution)/shard_map/ppermute | solution.py:471
  120.6 3.8 %collective-permute-done.8.one_side.g0 = f32[768,128]{1,0:T(8,128)S(1)} collective-permute-done((f32[768,128]{1,0:T(8,128)S(1)}, f32[768,128]{1,0:T(8,128)S(1)}, u32[]{:S(2)}, u32[]{:S(2)}) %collective-permute-start.8) | collective-permute-done | bytes 393248 | tf_op jit(solution)/shard_map/ppermute | solution.py:472
  124.4 0.8 copy-done.5
  125.2 3.4 %tiles_to_send.3 = (f32[576,128]{1,0:T(8,128)}, f32[576,128]{1,0:T(8,128)}) custom-call(s32[56,128]{1,0:T(8,128)} %get-tuple-element.23.lists, f32[768,128]{1,0:T(8,128)} %copy-done.5, f32[768,128]{1,0:T(8,128)} %copy-done.3, f32[768,128]{1,0:T(8,128)} %copy-done.4), custom_call_target="tpu_custom_call" | custom-call | tf_op jit(solution)/shard_map/tiles_to_send/pallas_call | solution.py:336
  128.6 1.9 %collective-permute-start.10 = (f32[576,128]{1,0:T(8,128)}, f32[576,128]{1,0:T(8,128)S(1)}, u32[]{:S(2)}, u32[]{:S(2)}) collective-permute-start(f32[576,128]{1,0:T(8,128)} %get-tuple-element.38), channel_id=1, source_target_pairs={{0,32},{32,0},{64,96},{96,64},{1,33},{33,1},{65,97},{97,65},{2,34}... | collective-permute-start | bytes 884744 | tf_op jit(solution)/shard_map/ppermute | solution.py:472
  130.5 4.5 %collective-permute-start.11 = (f32[576,128]{1,0:T(8,128)}, f32[576,128]{1,0:T(8,128)S(1)}, u32[]{:S(2)}, u32[]{:S(2)}) collective-permute-start(f32[576,128]{1,0:T(8,128)} %get-tuple-element.39), channel_id=1, source_target_pairs={{0,96},{32,64},{64,32},{96,0},{1,97},{33,65},{65,33},{97,1},{2,98}... | collective-permute-start | bytes 884744 | tf_op jit(solution)/shard_map/ppermute | solution.py:471
  135.9 1.0 copy.32
  136.9 1.1 pad.17.r_near
  138.0 5.1 %collective-permute-done.11.g4 = f32[576,128]{1,0:T(8,128)S(1)} collective-permute-done((f32[576,128]{1,0:T(8,128)}, f32[576,128]{1,0:T(8,128)S(1)}, u32[]{:S(2)}, u32[]{:S(2)}) %collective-permute-start.11) | collective-permute-done | bytes 294944 | tf_op jit(solution)/shard_map/ppermute | solution.py:471
  143.8 15.1 %pair_gradients.1 = (f32[256,128]{1,0:T(8,128)}, f32[8,256]{1,0:T(8,128)}) custom-call(s32[8,128]{1,0:T(8,128)} %get-tuple-element.27.count, s32[1,1792]{1,0:T(1,128)} %get-tuple-element.28.order, s32[1,1792]{1,0:T(1,128)} %get-tuple-element.29.own_rows, s32[1,1792]{1,0:T(1,128)} %get-tuple-element.30.other_rows, bf16[57344,128]{1,0:T(8,128)(2,1)} %get-tuple-element.32.filt, ...), custom_call_target="tpu_custom_call" | custom-call | tf_op jit(solution)/shard_map/pair_gradients/pallas_call | solution.py:451
  (53 shorter events, 8.8 us)
Async XLA Ops:
  0.6 134.4 %copy-start.12 = (f32[1,1,1,3,256]{4,2,3,1,0:T(1,128)S(1)}, f32[1,1,1,3,256]{4,2,3,1,0:T(1,128)}, u32[]{:S(2)}) copy-start(f32[1,1,1,3,256]{4,2,3,1,0:T(1,128)} %param.22) | copy-start | bytes 9220
  4.1 139.0 %copy-start.6 = (f32[256,128]{1,0:T(8,128)}, f32[256,128]{1,0:T(8,128)S(1)}, u32[]{:S(2)}) copy-start(f32[256,128]{1,0:T(8,128)S(1)} %fusion.6.own_h) | copy-start | bytes 393220
  4.2 17.8 %collective-permute-start.1 = (f32[1,264,128]{2,1,0:T(8,128)S(1)}, f32[1,264,128]{2,1,0:T(8,128)S(1)}, u32[]{:S(2)}, u32[]{:S(2)}) collective-permute-start(f32[1,264,128]{2,1,0:T(8,128)S(1)} %maximum_bitcast_fusion), channel_id=1, source_target_pairs={{0,31},{1,2},{2,1},{3,4},{4,3},{5,6},{6,5},{7,8},{8,7},{9,10},{10,... | collective-permute-start | bytes 405512 | tf_op jit(solution)/shard_map/ppermute | solution.py:471
  18.9 3.2 %collective-permute-start = (f32[1,264,128]{2,1,0:T(8,128)S(1)}, f32[1,264,128]{2,1,0:T(8,128)S(1)}, u32[]{:S(2)}, u32[]{:S(2)}) collective-permute-start(f32[1,264,128]{2,1,0:T(8,128)S(1)} %maximum_bitcast_fusion), channel_id=1, source_target_pairs={{0,1},{1,0},{2,3},{3,2},{4,5},{5,4},{6,7},{7,6},{8,9},{9,8},{10,11... | collective-permute-start | bytes 405512 | tf_op jit(solution)/shard_map/ppermute | solution.py:472
  22.2 27.7 %copy-start = (f32[3,256,128]{2,1,0:T(8,128)}, f32[3,256,128]{2,1,0:T(8,128)S(1)}, u32[]{:S(2)}) copy-start(f32[3,256,128]{2,1,0:T(8,128)S(1)} %pad_maximum_fusion) | copy-start | bytes 1179652
  22.2 27.7 %collective-permute-start.3 = (f32[768,128]{1,0:T(8,128)S(1)}, f32[768,128]{1,0:T(8,128)S(1)}, u32[]{:S(2)}, u32[]{:S(2)}) collective-permute-start(f32[768,128]{1,0:T(8,128)S(1)} %bitcast.37), channel_id=1, source_target_pairs={{0,384},{128,256},{256,128},{384,0},{1,385},{129,257},{257,129},{3... | collective-permute-start | bytes 1179656 | tf_op jit(solution)/shard_map/ppermute | solution.py:471
  25.6 24.3 %collective-permute-start.2 = (f32[768,128]{1,0:T(8,128)S(1)}, f32[768,128]{1,0:T(8,128)S(1)}, u32[]{:S(2)}, u32[]{:S(2)}) collective-permute-start(f32[768,128]{1,0:T(8,128)S(1)} %bitcast.38), channel_id=1, source_target_pairs={{0,128},{128,0},{256,384},{384,256},{1,129},{129,1},{257,385},{385... | collective-permute-start | bytes 1179656 | tf_op jit(solution)/shard_map/ppermute | solution.py:472
  30.0 11.2 %all-to-all-start = ((f32[16,24,128]{2,1,0:T(8,128)}), f32[16,24,128]{2,1,0:T(8,128)S(1)}, u32[]{:S(2)}, u32[]{:S(2)}) async-start(f32[16,24,128]{2,1,0:T(8,128)} %broadcast_in_dim.32), calls=%async_computation | async-start | bytes 393216 | tf_op jit(solution)/shard_map/all_to_all | solution.py:522
  49.9 85.9 %copy-start.11 = (f32[64,128]{1,0:T(8,128)S(1)}, f32[64,128]{1,0:T(8,128)}, u32[]{:S(2)}) copy-start(f32[64,128]{1,0:T(8,128)} %get-tuple-element.40) | copy-start | bytes 98308
  49.9 0.8 copy-start.1
  49.9 0.9 copy-start.2
  54.2 31.8 %collective-permute-start.4 = (f32[576,128]{1,0:T(8,128)}, f32[576,128]{1,0:T(8,128)S(1)}, u32[]{:S(2)}, u32[]{:S(2)}) collective-permute-start(f32[576,128]{1,0:T(8,128)} %get-tuple-element.33), channel_id=1, source_target_pairs={{0,32},{32,0},{64,96},{96,64},{1,33},{33,1},{65,97},{97,65},{2,34}... | collective-permute-start | bytes 884744 | tf_op jit(solution)/shard_map/ppermute | solution.py:472
  58.2 27.9 %collective-permute-start.5 = (f32[576,128]{1,0:T(8,128)}, f32[576,128]{1,0:T(8,128)S(1)}, u32[]{:S(2)}, u32[]{:S(2)}) collective-permute-start(f32[576,128]{1,0:T(8,128)} %get-tuple-element.34), channel_id=1, source_target_pairs={{0,96},{32,64},{64,32},{96,0},{1,97},{33,65},{65,33},{97,1},{2,98}... | collective-permute-start | bytes 884744 | tf_op jit(solution)/shard_map/ppermute | solution.py:471
  86.0 0.7 copy-start.7
  86.0 0.8 copy-start.8
  96.5 3.8 %collective-permute-start.6 = (f32[256,128]{1,0:T(8,128)}, f32[256,128]{1,0:T(8,128)S(1)}, u32[]{:S(2)}, u32[]{:S(2)}) collective-permute-start(f32[256,128]{1,0:T(8,128)} %get-tuple-element.37.own_g), channel_id=1, source_target_pairs={{0,1},{1,0},{2,3},{3,2},{4,5},{5,4},{6,7},{7,6},{8,9},{9,8},{10,11... | collective-permute-start | bytes 393224 | tf_op jit(solution)/shard_map/ppermute | solution.py:472
  98.4 12.5 %collective-permute-start.7 = (f32[256,128]{1,0:T(8,128)}, f32[256,128]{1,0:T(8,128)S(1)}, u32[]{:S(2)}, u32[]{:S(2)}) collective-permute-start(f32[256,128]{1,0:T(8,128)} %get-tuple-element.37.own_g), channel_id=1, source_target_pairs={{0,31},{1,2},{2,1},{3,4},{4,3},{5,6},{6,5},{7,8},{8,7},{9,10},{10,... | collective-permute-start | bytes 393224 | tf_op jit(solution)/shard_map/ppermute | solution.py:471
  111.0 13.5 %copy-start.3 = (f32[768,128]{1,0:T(8,128)}, f32[768,128]{1,0:T(8,128)S(1)}, u32[]{:S(2)}) copy-start(f32[768,128]{1,0:T(8,128)S(1)} %constant_dynamic-update-slice_fusion.middle.g1) | copy-start | bytes 1179652
  111.0 9.7 %collective-permute-start.9 = (f32[768,128]{1,0:T(8,128)S(1)}, f32[768,128]{1,0:T(8,128)S(1)}, u32[]{:S(2)}, u32[]{:S(2)}) collective-permute-start(f32[768,128]{1,0:T(8,128)S(1)} %constant_dynamic-update-slice_fusion.middle.g1), channel_id=1, source_target_pairs={{0,384},{128,256},{256,128},{384,0},{1,385},{129,257},{257,129},{3... | collective-permute-start | bytes 1179656 | tf_op jit(solution)/shard_map/ppermute | solution.py:471
  114.7 9.7 %collective-permute-start.8 = (f32[768,128]{1,0:T(8,128)S(1)}, f32[768,128]{1,0:T(8,128)S(1)}, u32[]{:S(2)}, u32[]{:S(2)}) collective-permute-start(f32[768,128]{1,0:T(8,128)S(1)} %constant_dynamic-update-slice_fusion.middle.g1), channel_id=1, source_target_pairs={{0,128},{128,0},{256,384},{384,256},{1,129},{129,1},{257,385},{385... | collective-permute-start | bytes 1179656 | tf_op jit(solution)/shard_map/ppermute | solution.py:472
  120.6 3.8 %copy-start.4 = (f32[768,128]{1,0:T(8,128)}, f32[768,128]{1,0:T(8,128)S(1)}, u32[]{:S(2)}) copy-start(f32[768,128]{1,0:T(8,128)S(1)} %collective-permute-done.9.other_side.g2) | copy-start | bytes 1179652
  124.4 0.8 copy-start.5
  128.6 9.4 %collective-permute-start.10 = (f32[576,128]{1,0:T(8,128)}, f32[576,128]{1,0:T(8,128)S(1)}, u32[]{:S(2)}, u32[]{:S(2)}) collective-permute-start(f32[576,128]{1,0:T(8,128)} %get-tuple-element.38), channel_id=1, source_target_pairs={{0,32},{32,0},{64,96},{96,64},{1,33},{33,1},{65,97},{97,65},{2,34}... | collective-permute-start | bytes 884744 | tf_op jit(solution)/shard_map/ppermute | solution.py:472
  130.5 12.5 %collective-permute-start.11 = (f32[576,128]{1,0:T(8,128)}, f32[576,128]{1,0:T(8,128)S(1)}, u32[]{:S(2)}, u32[]{:S(2)}) collective-permute-start(f32[576,128]{1,0:T(8,128)} %get-tuple-element.39), channel_id=1, source_target_pairs={{0,96},{32,64},{64,32},{96,0},{1,97},{33,65},{65,33},{97,1},{2,98}... | collective-permute-start | bytes 884744 | tf_op jit(solution)/shard_map/ppermute | solution.py:471
  138.0 5.1 %copy-start.9 = (f32[576,128]{1,0:T(8,128)}, f32[576,128]{1,0:T(8,128)S(1)}, u32[]{:S(2)}) copy-start(f32[576,128]{1,0:T(8,128)S(1)} %collective-permute-done.10.g3) | copy-start | bytes 884740
  143.1 0.7 copy-start.10

commit v3 on v2

--- a/solution.py
+++ b/solution.py
@@ -132,7 +132,7 @@
     place = [base[:, n : n + 1] + base[:, 2:3] * tiles[2 + n] for n in range(2)]
     listed = jnp.where(lane < 1, tiles[0], jnp.where(lane < 2, tiles[1], place[1]))
     listed = jnp.where(lane == 2, place[0], listed)
-    lists[...] = jnp.round(listed).astype(jnp.int32)
+    lists[...] = jnp.round(listed.T[0:8, :]).astype(jnp.int32)
 
     slot = lax.broadcasted_iota(jnp.int32, (SLOT_ROWS, 1), 0)
     halves = []
@@ -154,7 +154,8 @@
             rest = jnp.where(lane[0:SLOT_ROWS, 0:TILE] == q + 1, value, rest)
         halves.append(jnp.concatenate([*at, rest], axis=1))
     per_unit = jnp.concatenate(halves, axis=0)
-    at_unit[...] = per_unit
+    one_beside = lax.broadcasted_iota(jnp.int32, (2 * SLOT_ROWS, 128), 1) >= 96
+    at_unit[...] = jnp.where(one_beside, 1.0, per_unit)
     per_slab = jnp.dot(in_thirds(per_unit.T), units[...], preferred_element_type=f32)
 
     slab = lax.broadcasted_iota(jnp.int32, (TILE, WIDE), 1)
@@ -231,7 +232,7 @@
     outs = [
         jax.ShapeDtypeStruct((128, WIDE), jnp.float32),
         *[jax.ShapeDtypeStruct((1, SLABS), jnp.int32)] * 3,
-        jax.ShapeDtypeStruct((LIST_ROWS, 128), jnp.int32),
+        jax.ShapeDtypeStruct((8, LIST_ROWS), jnp.int32),
         jax.ShapeDtypeStruct((8, 128), jnp.int32),
         jax.ShapeDtypeStruct((2 * SLOT_ROWS, 128), jnp.float32),
     ]
@@ -257,8 +258,18 @@
     return jnp.clip(count[0, 0] - step * STEP, 0, STEP)
 
 
-def filter_kernel(count, order, table, centres, first_w, second_w, first_b, second_b, out, out_d):
+def filter_kernel(
+    count, order, table, centres, first_128, second_128, first_b, second_b, out, out_d, first_w, second_w
+):
     step = pl.program_id(0)
+
+    @pl.when(step == 0)
+    def _():
+        for wide_w, weight in ((first_w, first_128), (second_w, second_128)):
+            wide_w[...] = jnp.zeros_like(wide_w)
+            wide_w[0:128, 0:128] = weight[...]
+            wide_w[128:256, 128:256] = weight[...]
+
 
     def one(index, carry):
         spread = [[], [], [], []]
@@ -302,6 +313,7 @@
             grid=(STEPS,),
             in_specs=[whole(a) for a in arrays],
             out_specs=[wide, wide],
+            scratch_shapes=[pltpu.VMEM((256, 256), jnp.bfloat16)] * 2,
         ),
         out_shape=[jax.ShapeDtypeStruct((SLABS * TILE, 128), jnp.bfloat16)] * 2,
         compiler_params=pltpu.CompilerParams(vmem_limit_bytes=VMEM),
@@ -320,8 +332,8 @@
     laid_end_to_end((one_side, middle, other_side), held)
 
     def one(index, carry):
-        a = pl.multiple_of(lists[SLOT_ROWS + (index >> 1), 2 + (index & 1)], TILE)
-        b = pl.multiple_of(lists[SLOT_ROWS + 9 + (index >> 1), 2 + (index & 1)], TILE)
+        a = pl.multiple_of(lists[2 + (index & 1), SLOT_ROWS + (index >> 1)], TILE)
+        b = pl.multiple_of(lists[2 + (index & 1), SLOT_ROWS + 9 + (index >> 1)], TILE)
         o = pl.multiple_of(index * TILE, TILE)
         near[pl.ds(o, TILE), :] = held[pl.ds(a, TILE), :]
         far[pl.ds(o, TILE), :] = held[pl.ds(b, TILE), :]
@@ -433,8 +445,7 @@
         )
         for j, (own, slab) in enumerate(places):
             push = pushes[j % CHAINS]
-            away = r_near[pl.ds(slab, 1), :] - r_own[own, :]
-            push[own, :] = push[own, :] + sums[j * TILE : (j + 1) * TILE, :] * away
+            push[own, :] = push[own, :] + sums[j * TILE : (j + 1) * TILE, :] * r_near[pl.ds(slab, 1), :]
         return carry
 
     lax.fori_loop(0, bodies_of(step, count), one, 0)
@@ -443,7 +454,8 @@
     def _():
         cast = sum(total[...] for total in totals).astype(jnp.bfloat16)
         grad[...] = cot[...].astype(jnp.float32) + nt_dot(cast, in_w[...])
-        force[...] = sum(push[...] for push in pushes).T[0:8, :]
+        moments = sum(push[...] for push in pushes).T
+        force[...] = moments[0:3, :] - r_own[...] * moments[3:4, :]
 
 
 def pair_call(body, scalars, streams, arrays, outs, tables, scratch, name):
@@ -480,13 +492,6 @@
 def columns(three):
     near, far = swapped(three, three, "gx")
     return [near, three, far]
-
-
-def block_diagonal(weight):
-    zero = jnp.zeros_like(weight)
-    return jnp.concatenate(
-        [jnp.concatenate([weight, zero], axis=1), jnp.concatenate([zero, weight], axis=1)], axis=0
-    )
 
 
 def on_device(
@@ -551,8 +556,8 @@
         count,
         order,
         table,
-        block_diagonal(radial_weight),
-        block_diagonal(filter_weight),
+        radial_weight,
+        filter_weight,
         radial_bias[None],
         filter_bias[None],
     )
@@ -582,17 +587,16 @@
     g_x = columns(planes(d_msg))
     to_near, to_far = gather_tiles(lists, g_x)
     g_near = [*g_x, *swapped(to_far, to_near, "gy")]
-    r_near = at_unit[:, :96].reshape(2 * SLOT_ROWS, 3, TILE).transpose(0, 2, 1).reshape(WIDE, 3)
-    r_near = jnp.pad(r_near, ((0, 0), (0, 125)))
-    r_own = jnp.pad(own_pos.T, ((0, 0), (0, 125)))
+    r_near = at_unit.reshape(2 * SLOT_ROWS, 4, TILE).transpose(0, 2, 1).reshape(WIDE, 4)
+    r_near = jnp.pad(r_near, ((0, 0), (0, 124)))
     grad_features, force = pair_call(
         back_kernel,
         scalars,
         [filt, filt_d],
-        [*near, *g_near, hidden, d_msg, r_near, r_own, cot, input_weight],
+        [*near, *g_near, hidden, d_msg, r_near, own_pos, cot, input_weight],
         [
             jax.ShapeDtypeStruct((256, 128), jnp.float32),
-            jax.ShapeDtypeStruct((8, 256), jnp.float32),
+            jax.ShapeDtypeStruct((3, 256), jnp.float32),
         ],
         2,
         2 * CHAINS,
@@ -601,7 +605,7 @@
     return (
         new_features.reshape(1, 1, 1, 256, 128),
         grad_features.reshape(1, 1, 1, 256, 128),
-        force[:3].reshape(1, 1, 1, 3, 256),
+        force.reshape(1, 1, 1, 3, 256),
     )
 
 

time: 162 us -> 158 us (0.975)
  the two profiles are of different devices: /device:TPU:10 before, /device:TPU:8 now
where the time goes in v3:
time: 158 us; the launch traced here: 157 us
  Pallas kernels  59.7 us (38%)
  starting transfers between devices  56.8 us (36%)
  waiting for transfers between devices  25 us (16%)
  local copies, waits for them, and re-layouts  11.4 us (7%)
    ppermute x6, starting transfers between devices, swapped(): from_far = lax.ppermute(to_far, axis, far)  37.1 us
    pallas_call x2, Pallas kernels, pair_call(): pl.pallas_call(body, grid_spec=pltpu.PrefetchScalarGridSpec(num_scalar_pr...  23 us
    pallas_call x1, Pallas kernels, filters(): pl.pallas_call(filter_kernel, grid_spec=pltpu.PrefetchScalarGridSpec(num_...  22.7 us
    ppermute x6, waiting for transfers between devices, swapped(): from_far = lax.ppermute(to_far, axis, far)  16.9 us
    ppermute x6, starting transfers between devices, swapped(): return (lax.ppermute(to_near, axis, near), from_far)  14.1 us
    pallas_call x1, Pallas kernels, prepare(): pl.pallas_call(prepare_kernel, grid_spec=pltpu.PrefetchScalarGridSpec(num...  7.94 us
    unnamed x31, local copies, waits for them, and re-layouts  6.84 us
    all_to_all x1, waiting for transfers between devices, on_device(): lax.all_to_all(jnp.broadcast_to(meta_three.reshape(1, 24, 128), (along *...  6.41 us
  transfers between devices with their start and end apart: 13, of which 8 were waited for; matrix products, arithmetic and copies ran while one was open for 4% of the time, Pallas kernels for 20%

profile of v3, /device:TPU:8, one launch (start us, length us, event | category | flops | bytes accessed | tf_op | source)
XLA Modules:
  0.0 157.0 jit_solution(4655152825719732042)
XLA Ops:
  2.0 0.8 copy.28
  3.1 1.0 fusion.own_h
  4.2 14.7 %collective-permute-start.1 = (f32[1,264,128]{2,1,0:T(8,128)S(1)}, f32[1,264,128]{2,1,0:T(8,128)S(1)}, u32[]{:S(2)}, u32[]{:S(2)}) collective-permute-start(f32[1,264,128]{2,1,0:T(8,128)S(1)} %maximum_bitcast_fusion), channel_id=1, source_target_pairs={{0,31},{1,2},{2,1},{3,4},{4,3},{5,6},{6,5},{7,8},{8,7},{9,10},{10,... | collective-permute-start | bytes 405512 | tf_op jit(solution)/shard_map/ppermute | solution.py:483
  18.9 1.9 %collective-permute-start = (f32[1,264,128]{2,1,0:T(8,128)S(1)}, f32[1,264,128]{2,1,0:T(8,128)S(1)}, u32[]{:S(2)}, u32[]{:S(2)}) collective-permute-start(f32[1,264,128]{2,1,0:T(8,128)S(1)} %maximum_bitcast_fusion), channel_id=1, source_target_pairs={{0,1},{1,0},{2,3},{3,2},{4,5},{5,4},{6,7},{7,6},{8,9},{9,8},{10,11... | collective-permute-start | bytes 405512 | tf_op jit(solution)/shard_map/ppermute | solution.py:484
  20.9 1.1 collective-permute-done.1
  22.2 4.7 %collective-permute-start.3 = (f32[768,128]{1,0:T(8,128)S(1)}, f32[768,128]{1,0:T(8,128)S(1)}, u32[]{:S(2)}, u32[]{:S(2)}) collective-permute-start(f32[768,128]{1,0:T(8,128)S(1)} %bitcast.35), channel_id=1, source_target_pairs={{0,384},{128,256},{256,128},{384,0},{1,385},{129,257},{257,129},{3... | collective-permute-start | bytes 1179656 | tf_op jit(solution)/shard_map/ppermute | solution.py:483
  26.9 2.1 %collective-permute-start.2 = (f32[768,128]{1,0:T(8,128)S(1)}, f32[768,128]{1,0:T(8,128)S(1)}, u32[]{:S(2)}, u32[]{:S(2)}) collective-permute-start(f32[768,128]{1,0:T(8,128)S(1)} %bitcast.36), channel_id=1, source_target_pairs={{0,128},{128,0},{256,384},{384,256},{1,129},{129,1},{257,385},{385... | collective-permute-start | bytes 1179656 | tf_op jit(solution)/shard_map/ppermute | solution.py:484
  29.7 5.7 %all-to-all-start = ((f32[16,24,128]{2,1,0:T(8,128)}), f32[16,24,128]{2,1,0:T(8,128)S(1)}, u32[]{:S(2)}, u32[]{:S(2)}) async-start(f32[16,24,128]{2,1,0:T(8,128)} %broadcast_in_dim.32), calls=%async_computation | async-start | bytes 393216 | tf_op jit(solution)/shard_map/all_to_all | solution.py:527
  36.8 6.4 %all-to-all-done = f32[16,24,128]{2,1,0:T(8,128)S(1)} async-done(((f32[16,24,128]{2,1,0:T(8,128)}), f32[16,24,128]{2,1,0:T(8,128)S(1)}, u32[]{:S(2)}, u32[]{:S(2)}) %all-to-all-start) | async-done | bytes 196640 | tf_op jit(solution)/shard_map/all_to_all | solution.py:527
  43.2 0.7 reshape_reshape.11.everyone
  43.9 7.9 %distances_and_live_rows.1 = (f32[128,2048]{1,0:T(8,128)}, s32[1,1792]{1,0:T(1,128)}, s32[1,1792]{1,0:T(1,128)}, s32[1,1792]{1,0:T(1,128)}, s32[8,56]{1,0:T(8,12...) custom-call(s32[3]{0:T(128)} %pad_add_fusion.where, f32[48,1024]{1,0:T(8,128)} %reshape_reshape.11.everyone, ...), custom_call_target="tpu_custom_call" | custom-call | tf_op jit(solution)/shard_map/distances_and_live_rows/pallas_call | solution.py:239
  52.8 3.1 %tiles_to_send.2 = (f32[576,128]{1,0:T(8,128)}, f32[576,128]{1,0:T(8,128)}) custom-call(s32[8,56]{1,0:T(8,128)} %get-tuple-element.23.lists, f32[768,128]{1,0:T(8,128)} %copy-done.2, f32[768,128]{1,0:T(8,128)} %bitcast.37, f32[768,128]{1,0:T(8,128)} %copy-done.1), custom_call_target="tpu_custom_call" | custom-call | tf_op jit(solution)/shard_map/tiles_to_send/pallas_call | solution.py:348
  55.9 2.9 %collective-permute-start.4 = (f32[576,128]{1,0:T(8,128)}, f32[576,128]{1,0:T(8,128)S(1)}, u32[]{:S(2)}, u32[]{:S(2)}) collective-permute-start(f32[576,128]{1,0:T(8,128)} %get-tuple-element.33), channel_id=1, source_target_pairs={{0,32},{32,0},{64,96},{96,64},{1,33},{33,1},{65,97},{97,65},{2,34}... | collective-permute-start | bytes 884744 | tf_op jit(solution)/shard_map/ppermute | solution.py:484
  58.7 2.0 %collective-permute-start.5 = (f32[576,128]{1,0:T(8,128)}, f32[576,128]{1,0:T(8,128)S(1)}, u32[]{:S(2)}, u32[]{:S(2)}) collective-permute-start(f32[576,128]{1,0:T(8,128)} %get-tuple-element.34), channel_id=1, source_target_pairs={{0,96},{32,64},{64,32},{96,0},{1,97},{33,65},{65,33},{97,1},{2,98}... | collective-permute-start | bytes 884744 | tf_op jit(solution)/shard_map/ppermute | solution.py:483
  60.8 22.7 %pair_filters.1 = (bf16[57344,128]{1,0:T(8,128)(2,1)}, bf16[57344,128]{1,0:T(8,128)(2,1)}) custom-call(s32[8,128]{1,0:T(8,128)} %get-tuple-element.27.count, s32[1,1792]{1,0:T(1,128)} %get-tuple-element.28.order, f32[128,2048]{1,0:T(8,128)} %get-tuple-element.31.table, f32[1,128]{1,0:T(1,128)} %constant.37.clone.centres, bf16[128,128]{1,0:T(8,128)(2,1)} %first_128.1, ...), custom_call_target="tpu_custom_call" | custom-call | tf_op jit(solution)/shard_map/pair_filters/pallas_call | solution.py:309
  84.4 8.8 %messages_and_update.1 = (bf16[256,128]{1,0:T(8,128)(2,1)}, f32[256,128]{1,0:T(8,128)}) custom-call(s32[8,128]{1,0:T(8,128)} %get-tuple-element.27.count, s32[1,1792]{1,0:T(1,128)} %get-tuple-element.28.order, s32[1,1792]{1,0:T(1,128)} %get-tuple-element.29.own_rows, s32[1,1792]{1,0:T(1,128)} %get-tuple-element.30.other_rows, ...), custom_call_target="tpu_custom_call" | custom-call | tf_op jit(solution)/shard_map/messages_and_update/pallas_call | solution.py:463
  93.1 1.9 %collective-permute-start.6 = (f32[256,128]{1,0:T(8,128)}, f32[256,128]{1,0:T(8,128)S(1)}, u32[]{:S(2)}, u32[]{:S(2)}) collective-permute-start(f32[256,128]{1,0:T(8,128)} %get-tuple-element.37.own_g), channel_id=1, source_target_pairs={{0,1},{1,0},{2,3},{3,2},{4,5},{5,4},{6,7},{7,6},{8,9},{9,8},{10,11... | collective-permute-start | bytes 393224 | tf_op jit(solution)/shard_map/ppermute | solution.py:484
  95.0 11.7 %collective-permute-start.7 = (f32[256,128]{1,0:T(8,128)}, f32[256,128]{1,0:T(8,128)S(1)}, u32[]{:S(2)}, u32[]{:S(2)}) collective-permute-start(f32[256,128]{1,0:T(8,128)} %get-tuple-element.37.own_g), channel_id=1, source_target_pairs={{0,31},{1,2},{2,1},{3,4},{4,3},{5,6},{6,5},{7,8},{8,7},{9,10},{10,... | collective-permute-start | bytes 393224 | tf_op jit(solution)/shard_map/ppermute | solution.py:483
  106.7 0.9 constant_dynamic-update-slice_fusion.1
  107.7 2.3 %collective-permute-done.7 = f32[256,128]{1,0:T(8,128)S(1)} collective-permute-done((f32[256,128]{1,0:T(8,128)}, f32[256,128]{1,0:T(8,128)S(1)}, u32[]{:S(2)}, u32[]{:S(2)}) %collective-permute-start.7) | collective-permute-done | bytes 131104 | tf_op jit(solution)/shard_map/ppermute | solution.py:483
  110.0 1.9 %collective-permute-start.9 = (f32[768,128]{1,0:T(8,128)S(1)}, f32[768,128]{1,0:T(8,128)S(1)}, u32[]{:S(2)}, u32[]{:S(2)}) collective-permute-start(f32[768,128]{1,0:T(8,128)S(1)} %constant_dynamic-update-slice_fusion.middle.g1), channel_id=1, source_target_pairs={{0,384},{128,256},{256,128},{384,0},{1,385},{129,257},{257,129},{3... | collective-permute-start | bytes 1179656 | tf_op jit(solution)/shard_map/ppermute | solution.py:483
  112.0 1.9 %collective-permute-start.8 = (f32[768,128]{1,0:T(8,128)S(1)}, f32[768,128]{1,0:T(8,128)S(1)}, u32[]{:S(2)}, u32[]{:S(2)}) collective-permute-start(f32[768,128]{1,0:T(8,128)S(1)} %constant_dynamic-update-slice_fusion.middle.g1), channel_id=1, source_target_pairs={{0,128},{128,0},{256,384},{384,256},{1,129},{129,1},{257,385},{385... | collective-permute-start | bytes 1179656 | tf_op jit(solution)/shard_map/ppermute | solution.py:484
  113.9 7.0 %collective-permute-done.9.other_side.g2 = f32[768,128]{1,0:T(8,128)S(1)} collective-permute-done((f32[768,128]{1,0:T(8,128)S(1)}, f32[768,128]{1,0:T(8,128)S(1)}, u32[]{:S(2)}, u32[]{:S(2)}) %collective-permute-start.9) | collective-permute-done | bytes 393248 | tf_op jit(solution)/shard_map/ppermute | solution.py:483
  121.7 0.8 copy-done.5
  122.4 3.0 %tiles_to_send.3 = (f32[576,128]{1,0:T(8,128)}, f32[576,128]{1,0:T(8,128)}) custom-call(s32[8,56]{1,0:T(8,128)} %get-tuple-element.23.lists, f32[768,128]{1,0:T(8,128)} %copy-done.5, f32[768,128]{1,0:T(8,128)} %copy-done.3, f32[768,128]{1,0:T(8,128)} %copy-done.4), custom_call_target="tpu_custom_call" | custom-call | tf_op jit(solution)/shard_map/tiles_to_send/pallas_call | solution.py:348
  125.5 3.3 %collective-permute-start.10 = (f32[576,128]{1,0:T(8,128)}, f32[576,128]{1,0:T(8,128)S(1)}, u32[]{:S(2)}, u32[]{:S(2)}) collective-permute-start(f32[576,128]{1,0:T(8,128)} %get-tuple-element.38), channel_id=1, source_target_pairs={{0,32},{32,0},{64,96},{96,64},{1,33},{33,1},{65,97},{97,65},{2,34}... | collective-permute-start | bytes 884744 | tf_op jit(solution)/shard_map/ppermute | solution.py:484
  128.8 2.0 %collective-permute-start.11 = (f32[576,128]{1,0:T(8,128)}, f32[576,128]{1,0:T(8,128)S(1)}, u32[]{:S(2)}, u32[]{:S(2)}) collective-permute-start(f32[576,128]{1,0:T(8,128)} %get-tuple-element.39), channel_id=1, source_target_pairs={{0,96},{32,64},{64,32},{96,0},{1,97},{33,65},{65,33},{97,1},{2,98}... | collective-permute-start | bytes 884744 | tf_op jit(solution)/shard_map/ppermute | solution.py:483
  131.6 1.0 copy.31
  132.5 1.1 pad.9.r_near
  134.3 6.5 %collective-permute-done.11.g4 = f32[576,128]{1,0:T(8,128)S(1)} collective-permute-done((f32[576,128]{1,0:T(8,128)}, f32[576,128]{1,0:T(8,128)S(1)}, u32[]{:S(2)}, u32[]{:S(2)}) %collective-permute-start.11) | collective-permute-done | bytes 294944 | tf_op jit(solution)/shard_map/ppermute | solution.py:483
  141.5 14.2 %pair_gradients.1 = (f32[256,128]{1,0:T(8,128)}, f32[3,256]{1,0:T(4,128)}) custom-call(s32[8,128]{1,0:T(8,128)} %get-tuple-element.27.count, s32[1,1792]{1,0:T(1,128)} %get-tuple-element.28.order, s32[1,1792]{1,0:T(1,128)} %get-tuple-element.29.own_rows, s32[1,1792]{1,0:T(1,128)} %get-tuple-element.30.other_rows, bf16[57344,128]{1,0:T(8,128)(2,1)} %get-tuple-element.32.filt, ...), custom_call_target="tpu_custom_call" | custom-call | tf_op jit(solution)/shard_map/pair_gradients/pallas_call | solution.py:463
  155.7 1.3 copy.32
  (50 shorter events, 8.0 us)
Async XLA Ops:
  0.6 130.2 %copy-start.12 = (f32[1,1,1,3,256]{4,2,3,1,0:T(1,128)S(1)}, f32[1,1,1,3,256]{4,2,3,1,0:T(1,128)}, u32[]{:S(2)}) copy-start(f32[1,1,1,3,256]{4,2,3,1,0:T(1,128)} %param.22) | copy-start | bytes 9220
  4.1 136.8 %copy-start.6 = (f32[256,128]{1,0:T(8,128)}, f32[256,128]{1,0:T(8,128)S(1)}, u32[]{:S(2)}) copy-start(f32[256,128]{1,0:T(8,128)S(1)} %fusion.own_h) | copy-start | bytes 393220
  4.2 17.8 %collective-permute-start.1 = (f32[1,264,128]{2,1,0:T(8,128)S(1)}, f32[1,264,128]{2,1,0:T(8,128)S(1)}, u32[]{:S(2)}, u32[]{:S(2)}) collective-permute-start(f32[1,264,128]{2,1,0:T(8,128)S(1)} %maximum_bitcast_fusion), channel_id=1, source_target_pairs={{0,31},{1,2},{2,1},{3,4},{4,3},{5,6},{6,5},{7,8},{8,7},{9,10},{10,... | collective-permute-start | bytes 405512 | tf_op jit(solution)/shard_map/ppermute | solution.py:483
  18.9 3.2 %collective-permute-start = (f32[1,264,128]{2,1,0:T(8,128)S(1)}, f32[1,264,128]{2,1,0:T(8,128)S(1)}, u32[]{:S(2)}, u32[]{:S(2)}) collective-permute-start(f32[1,264,128]{2,1,0:T(8,128)S(1)} %maximum_bitcast_fusion), channel_id=1, source_target_pairs={{0,1},{1,0},{2,3},{3,2},{4,5},{5,4},{6,7},{7,6},{8,9},{9,8},{10,11... | collective-permute-start | bytes 405512 | tf_op jit(solution)/shard_map/ppermute | solution.py:484
  22.2 29.7 %copy-start = (f32[3,256,128]{2,1,0:T(8,128)}, f32[3,256,128]{2,1,0:T(8,128)S(1)}, u32[]{:S(2)}) copy-start(f32[3,256,128]{2,1,0:T(8,128)S(1)} %pad_maximum_fusion) | copy-start | bytes 1179652
  22.2 29.7 %collective-permute-start.3 = (f32[768,128]{1,0:T(8,128)S(1)}, f32[768,128]{1,0:T(8,128)S(1)}, u32[]{:S(2)}, u32[]{:S(2)}) collective-permute-start(f32[768,128]{1,0:T(8,128)S(1)} %bitcast.35), channel_id=1, source_target_pairs={{0,384},{128,256},{256,128},{384,0},{1,385},{129,257},{257,129},{3... | collective-permute-start | bytes 1179656 | tf_op jit(solution)/shard_map/ppermute | solution.py:483
  26.9 25.0 %collective-permute-start.2 = (f32[768,128]{1,0:T(8,128)S(1)}, f32[768,128]{1,0:T(8,128)S(1)}, u32[]{:S(2)}, u32[]{:S(2)}) collective-permute-start(f32[768,128]{1,0:T(8,128)S(1)} %bitcast.36), channel_id=1, source_target_pairs={{0,128},{128,0},{256,384},{384,256},{1,129},{129,1},{257,385},{385... | collective-permute-start | bytes 1179656 | tf_op jit(solution)/shard_map/ppermute | solution.py:484
  29.7 13.5 %all-to-all-start = ((f32[16,24,128]{2,1,0:T(8,128)}), f32[16,24,128]{2,1,0:T(8,128)S(1)}, u32[]{:S(2)}, u32[]{:S(2)}) async-start(f32[16,24,128]{2,1,0:T(8,128)} %broadcast_in_dim.32), calls=%async_computation | async-start | bytes 393216 | tf_op jit(solution)/shard_map/all_to_all | solution.py:527
  51.9 79.6 %copy-start.11 = (f32[64,128]{1,0:T(8,128)S(1)}, f32[64,128]{1,0:T(8,128)}, u32[]{:S(2)}) copy-start(f32[64,128]{1,0:T(8,128)} %get-tuple-element.40) | copy-start | bytes 98308
  51.9 0.8 copy-start.1
  51.9 0.9 copy-start.2
  55.9 27.6 %collective-permute-start.4 = (f32[576,128]{1,0:T(8,128)}, f32[576,128]{1,0:T(8,128)S(1)}, u32[]{:S(2)}, u32[]{:S(2)}) collective-permute-start(f32[576,128]{1,0:T(8,128)} %get-tuple-element.33), channel_id=1, source_target_pairs={{0,32},{32,0},{64,96},{96,64},{1,33},{33,1},{65,97},{97,65},{2,34}... | collective-permute-start | bytes 884744 | tf_op jit(solution)/shard_map/ppermute | solution.py:484
  58.7 24.8 %collective-permute-start.5 = (f32[576,128]{1,0:T(8,128)}, f32[576,128]{1,0:T(8,128)S(1)}, u32[]{:S(2)}, u32[]{:S(2)}) collective-permute-start(f32[576,128]{1,0:T(8,128)} %get-tuple-element.34), channel_id=1, source_target_pairs={{0,96},{32,64},{64,32},{96,0},{1,97},{33,65},{65,33},{97,1},{2,98}... | collective-permute-start | bytes 884744 | tf_op jit(solution)/shard_map/ppermute | solution.py:483
  83.5 0.7 copy-start.7
  83.5 0.8 copy-start.8
  93.1 13.6 %collective-permute-start.6 = (f32[256,128]{1,0:T(8,128)}, f32[256,128]{1,0:T(8,128)S(1)}, u32[]{:S(2)}, u32[]{:S(2)}) collective-permute-start(f32[256,128]{1,0:T(8,128)} %get-tuple-element.37.own_g), channel_id=1, source_target_pairs={{0,1},{1,0},{2,3},{3,2},{4,5},{5,4},{6,7},{7,6},{8,9},{9,8},{10,11... | collective-permute-start | bytes 393224 | tf_op jit(solution)/shard_map/ppermute | solution.py:484
  95.0 15.0 %collective-permute-start.7 = (f32[256,128]{1,0:T(8,128)}, f32[256,128]{1,0:T(8,128)S(1)}, u32[]{:S(2)}, u32[]{:S(2)}) collective-permute-start(f32[256,128]{1,0:T(8,128)} %get-tuple-element.37.own_g), channel_id=1, source_target_pairs={{0,31},{1,2},{2,1},{3,4},{4,3},{5,6},{6,5},{7,8},{8,7},{9,10},{10,... | collective-permute-start | bytes 393224 | tf_op jit(solution)/shard_map/ppermute | solution.py:483
  110.0 11.6 %copy-start.3 = (f32[768,128]{1,0:T(8,128)}, f32[768,128]{1,0:T(8,128)S(1)}, u32[]{:S(2)}) copy-start(f32[768,128]{1,0:T(8,128)S(1)} %constant_dynamic-update-slice_fusion.middle.g1) | copy-start | bytes 1179652
  110.0 10.9 %collective-permute-start.9 = (f32[768,128]{1,0:T(8,128)S(1)}, f32[768,128]{1,0:T(8,128)S(1)}, u32[]{:S(2)}, u32[]{:S(2)}) collective-permute-start(f32[768,128]{1,0:T(8,128)S(1)} %constant_dynamic-update-slice_fusion.middle.g1), channel_id=1, source_target_pairs={{0,384},{128,256},{256,128},{384,0},{1,385},{129,257},{257,129},{3... | collective-permute-start | bytes 1179656 | tf_op jit(solution)/shard_map/ppermute | solution.py:483
  112.0 9.7 %collective-permute-start.8 = (f32[768,128]{1,0:T(8,128)S(1)}, f32[768,128]{1,0:T(8,128)S(1)}, u32[]{:S(2)}, u32[]{:S(2)}) collective-permute-start(f32[768,128]{1,0:T(8,128)S(1)} %constant_dynamic-update-slice_fusion.middle.g1), channel_id=1, source_target_pairs={{0,128},{128,0},{256,384},{384,256},{1,129},{129,1},{257,385},{385... | collective-permute-start | bytes 1179656 | tf_op jit(solution)/shard_map/ppermute | solution.py:484
  120.9 0.8 copy-start.4
  121.7 0.8 copy-start.5
  125.5 8.8 %collective-permute-start.10 = (f32[576,128]{1,0:T(8,128)}, f32[576,128]{1,0:T(8,128)S(1)}, u32[]{:S(2)}, u32[]{:S(2)}) collective-permute-start(f32[576,128]{1,0:T(8,128)} %get-tuple-element.38), channel_id=1, source_target_pairs={{0,32},{32,0},{64,96},{96,64},{1,33},{33,1},{65,97},{97,65},{2,34}... | collective-permute-start | bytes 884744 | tf_op jit(solution)/shard_map/ppermute | solution.py:484
  128.8 12.0 %collective-permute-start.11 = (f32[576,128]{1,0:T(8,128)}, f32[576,128]{1,0:T(8,128)S(1)}, u32[]{:S(2)}, u32[]{:S(2)}) collective-permute-start(f32[576,128]{1,0:T(8,128)} %get-tuple-element.39), channel_id=1, source_target_pairs={{0,96},{32,64},{64,32},{96,0},{1,97},{33,65},{65,33},{97,1},{2,98}... | collective-permute-start | bytes 884744 | tf_op jit(solution)/shard_map/ppermute | solution.py:483
  134.3 6.5 %copy-start.9 = (f32[576,128]{1,0:T(8,128)}, f32[576,128]{1,0:T(8,128)S(1)}, u32[]{:S(2)}) copy-start(f32[576,128]{1,0:T(8,128)S(1)} %collective-permute-done.10.g3) | copy-start | bytes 884740
  140.8 0.7 copy-start.10

commit v4 on v3

--- a/solution.py
+++ b/solution.py
@@ -112,7 +112,7 @@
 
 
 def prepare_kernel(
-    where, everyone, holders, lanes, bases, side, shift, own_side, units,
+    where, everyone, holders, lanes, bases, side, shift, own_side,
     table, order, own_rows, other_rows, lists, count, at_unit
 ):
     f32 = jnp.float32
@@ -156,7 +156,12 @@
     per_unit = jnp.concatenate(halves, axis=0)
     one_beside = lax.broadcasted_iota(jnp.int32, (2 * SLOT_ROWS, 128), 1) >= 96
     at_unit[...] = jnp.where(one_beside, 1.0, per_unit)
-    per_slab = jnp.dot(in_thirds(per_unit.T), units[...], preferred_element_type=f32)
+    unit = lax.broadcasted_iota(jnp.int32, (2 * SLOT_ROWS, WIDE), 0)
+    slab = lax.broadcasted_iota(jnp.int32, (2 * SLOT_ROWS, WIDE), 1)
+    units = jnp.where(unit == (slab >> 5), 1.0, 0.0).astype(jnp.bfloat16)
+    per_slab = jnp.dot(
+        in_thirds(per_unit.T), jnp.concatenate([units] * 3, axis=0), preferred_element_type=f32
+    )
 
     slab = lax.broadcasted_iota(jnp.int32, (TILE, WIDE), 1)
     u = lax.broadcasted_iota(jnp.int32, (TILE, WIDE), 0)
@@ -201,19 +206,22 @@
     total = before[blocks - 1 : blocks, :] + until[blocks - 1 : blocks, 127:128]
     bodies = jnp.floor((total + (BODY - 1.0)) * (1.0 / BODY))
     count[...] = jnp.broadcast_to(bodies, (8, 128)).astype(jnp.int32)
-    target = lax.broadcasted_iota(jnp.int32, (SLABS, 256), 0).astype(f32)
+    target = lax.broadcasted_iota(jnp.int32, (256, 256), 0).astype(f32)
     names_row = lax.broadcasted_iota(jnp.int32, (8, 256), 0)
     names_lane = lax.broadcasted_iota(jnp.int32, (8, 256), 1)
-    found = jnp.zeros((8, SLABS), f32)
+    found = [jnp.zeros((8, 256), f32)] * (SLABS // 256)
     for b in range(blocks // 2):
         wide_rank = jnp.concatenate([rank[2 * b : 2 * b + 1], rank[2 * b + 1 : 2 * b + 2]], axis=1)
-        hit = jnp.where(target == wide_rank, 1.0, 0.0).astype(jnp.bfloat16)
         names = jnp.where(names_row == 0, b * 8 + (names_lane >> 5), names_lane & (TILE - 1))
         names = jnp.where(names_row == 2, 1, names).astype(f32)
         part = slice(b * 256, (b + 1) * 256)
         names = jnp.where(names_row == 3, per_slab[96:97, part], names)
         names = jnp.where(names_row == 4, per_slab[100:101, part], names)
-        found = found + nt_dot(names.astype(jnp.bfloat16), hit)
+        names = names.astype(jnp.bfloat16)
+        for i in range(min(b + 1, len(found))):
+            hit = jnp.where(target == wide_rank - i * 256.0, 1.0, 0.0).astype(jnp.bfloat16)
+            found[i] = found[i] + nt_dot(names, hit)
+    found = jnp.concatenate(found, axis=1)
     named = jnp.where(found[2:3] > 0.5, found[0:1] * TILE + found[1:2], 1.0 * IDLE)
     order[...] = jnp.round(named).astype(jnp.int32)
     own_rows[...] = jnp.round(found[3:4] * TILE).astype(jnp.int32)
@@ -536,7 +544,6 @@
     sides[:28, :3] = side
     sides[:28, 3] = 1
     selectors = [list_selectors((-1, 1)), list_selectors((1, -1))]
-    units = np.arange(WIDE)[None] // TILE == np.arange(2 * SLOT_ROWS)[:, None]
     where = jnp.stack([lax.axis_index(axis) for axis in ("gx", "gy", "gz")]).astype(jnp.int32)
     table, order, own_rows, other_rows, lists, count, at_unit = prepare(
         where,
@@ -547,7 +554,6 @@
         jnp.asarray(sides),
         jnp.asarray(sides[:, :3].astype(np.float32)),
         own_pos.reshape(3, 8, TILE).transpose(0, 2, 1).reshape(96, 8),
-        jnp.asarray(np.tile(units, (3, 1)).astype(jnp.bfloat16)),
     )
     near_x = columns(hidden_three)
     to_near, to_far, count = lax.optimization_barrier((*gather_tiles(lists, near_x), count))

time: 158 us -> 158 us (level)
  waiting for transfers between devices: 25 us -> 28.4 us
  starting transfers between devices: 56.8 us -> 53.8 us
    ppermute x6, starting transfers between devices: 37.1 us -> 32.1 us  [swapped(): from_far = lax.ppermute(to_far, axis, far)]
    ppermute x6, waiting for transfers between devices: 16.9 us -> 20.1 us  [swapped(): from_far = lax.ppermute(to_far, axis, far)]
    ppermute x6, starting transfers between devices: 14.1 us -> 16 us  [swapped(): return (lax.ppermute(to_near, axis, near), from_far)]
  transfers between devices with their start and end apart: 13 -> 13, of which waited for: 8 -> 7; matrix products, arithmetic and copies ran while one was open for 4% -> 4% of each run, Pallas kernels for 20% -> 19%
where the time goes in v4:
time: 158 us; the launch traced here: 156 us
  Pallas kernels  58.8 us (37%)
  starting transfers between devices  53.8 us (34%)
  waiting for transfers between devices  28.4 us (18%)
  local copies, waits for them, and re-layouts  11.4 us (7%)
    ppermute x6, starting transfers between devices, swapped(): from_far = lax.ppermute(to_far, axis, far)  32.1 us
    pallas_call x2, Pallas kernels, pair_call(): pl.pallas_call(body, grid_spec=pltpu.PrefetchScalarGridSpec(num_scalar_pr...  23 us
    pallas_call x1, Pallas kernels, filters(): pl.pallas_call(filter_kernel, grid_spec=pltpu.PrefetchScalarGridSpec(num_...  22.7 us
    ppermute x6, waiting for transfers between devices, swapped(): from_far = lax.ppermute(to_far, axis, far)  20.1 us
    ppermute x6, starting transfers between devices, swapped(): return (lax.ppermute(to_near, axis, near), from_far)  16 us
    pallas_call x1, Pallas kernels, prepare(): pl.pallas_call(prepare_kernel, grid_spec=pltpu.PrefetchScalarGridSpec(num...  6.99 us
    unnamed x31, local copies, waits for them, and re-layouts  6.8 us
    all_to_all x1, waiting for transfers between devices, on_device(): lax.all_to_all(jnp.broadcast_to(meta_three.reshape(1, 24, 128), (along *...  6.41 us
  transfers between devices with their start and end apart: 13, of which 7 were waited for; matrix products, arithmetic and copies ran while one was open for 4% of the time, Pallas kernels for 19%

profile of v4, /device:TPU:8, one launch (start us, length us, event | category | flops | bytes accessed | tf_op | source)
XLA Modules:
  0.0 156.4 jit_solution(7626108349337732703)
XLA Ops:
  2.0 0.8 copy.27
  3.1 1.0 fusion.own_h
  4.2 14.7 %collective-permute-start.1 = (f32[1,264,128]{2,1,0:T(8,128)S(1)}, f32[1,264,128]{2,1,0:T(8,128)S(1)}, u32[]{:S(2)}, u32[]{:S(2)}) collective-permute-start(f32[1,264,128]{2,1,0:T(8,128)S(1)} %maximum_bitcast_fusion), channel_id=1, source_target_pairs={{0,31},{1,2},{2,1},{3,4},{4,3},{5,6},{6,5},{7,8},{8,7},{9,10},{10,... | collective-permute-start | bytes 405512 | tf_op jit(solution)/shard_map/ppermute | solution.py:491
  18.9 1.9 %collective-permute-start = (f32[1,264,128]{2,1,0:T(8,128)S(1)}, f32[1,264,128]{2,1,0:T(8,128)S(1)}, u32[]{:S(2)}, u32[]{:S(2)}) collective-permute-start(f32[1,264,128]{2,1,0:T(8,128)S(1)} %maximum_bitcast_fusion), channel_id=1, source_target_pairs={{0,1},{1,0},{2,3},{3,2},{4,5},{5,4},{6,7},{7,6},{8,9},{9,8},{10,11... | collective-permute-start | bytes 405512 | tf_op jit(solution)/shard_map/ppermute | solution.py:492
  20.9 1.1 collective-permute-done.1
  22.2 4.7 %collective-permute-start.3 = (f32[768,128]{1,0:T(8,128)S(1)}, f32[768,128]{1,0:T(8,128)S(1)}, u32[]{:S(2)}, u32[]{:S(2)}) collective-permute-start(f32[768,128]{1,0:T(8,128)S(1)} %bitcast.35), channel_id=1, source_target_pairs={{0,384},{128,256},{256,128},{384,0},{1,385},{129,257},{257,129},{3... | collective-permute-start | bytes 1179656 | tf_op jit(solution)/shard_map/ppermute | solution.py:491
  26.9 2.1 %collective-permute-start.2 = (f32[768,128]{1,0:T(8,128)S(1)}, f32[768,128]{1,0:T(8,128)S(1)}, u32[]{:S(2)}, u32[]{:S(2)}) collective-permute-start(f32[768,128]{1,0:T(8,128)S(1)} %bitcast.36), channel_id=1, source_target_pairs={{0,128},{128,0},{256,384},{384,256},{1,129},{129,1},{257,385},{385... | collective-permute-start | bytes 1179656 | tf_op jit(solution)/shard_map/ppermute | solution.py:492
  29.7 5.7 %all-to-all-start = ((f32[16,24,128]{2,1,0:T(8,128)}), f32[16,24,128]{2,1,0:T(8,128)S(1)}, u32[]{:S(2)}, u32[]{:S(2)}) async-start(f32[16,24,128]{2,1,0:T(8,128)} %broadcast_in_dim.32), calls=%async_computation | async-start | bytes 393216 | tf_op jit(solution)/shard_map/all_to_all | solution.py:535
  36.8 6.4 %all-to-all-done = f32[16,24,128]{2,1,0:T(8,128)S(1)} async-done(((f32[16,24,128]{2,1,0:T(8,128)}), f32[16,24,128]{2,1,0:T(8,128)S(1)}, u32[]{:S(2)}, u32[]{:S(2)}) %all-to-all-start) | async-done | bytes 196640 | tf_op jit(solution)/shard_map/all_to_all | solution.py:535
  43.9 7.0 %distances_and_live_rows.1 = (f32[128,2048]{1,0:T(8,128)}, s32[1,1792]{1,0:T(1,128)}, s32[1,1792]{1,0:T(1,128)}, s32[1,1792]{1,0:T(1,128)}, s32[8,56]{1,0:T(8,12...) custom-call(s32[3]{0:T(128)} %pad_add_fusion.where, f32[48,1024]{1,0:T(8,128)} %reshape_reshape.11.everyone, ...), custom_call_target="tpu_custom_call" | custom-call | tf_op jit(solution)/shard_map/distances_and_live_rows/pallas_call | solution.py:247
  51.8 3.1 %tiles_to_send.2 = (f32[576,128]{1,0:T(8,128)}, f32[576,128]{1,0:T(8,128)}) custom-call(s32[8,56]{1,0:T(8,128)} %get-tuple-element.23.lists, f32[768,128]{1,0:T(8,128)} %copy-done.2, f32[768,128]{1,0:T(8,128)} %bitcast.37, f32[768,128]{1,0:T(8,128)} %copy-done.1), custom_call_target="tpu_custom_call" | custom-call | tf_op jit(solution)/shard_map/tiles_to_send/pallas_call | solution.py:356
  54.9 2.9 %collective-permute-start.4 = (f32[576,128]{1,0:T(8,128)}, f32[576,128]{1,0:T(8,128)S(1)}, u32[]{:S(2)}, u32[]{:S(2)}) collective-permute-start(f32[576,128]{1,0:T(8,128)} %get-tuple-element.33), channel_id=1, source_target_pairs={{0,32},{32,0},{64,96},{96,64},{1,33},{33,1},{65,97},{97,65},{2,34}... | collective-permute-start | bytes 884744 | tf_op jit(solution)/shard_map/ppermute | solution.py:492
  57.8 2.0 %collective-permute-start.5 = (f32[576,128]{1,0:T(8,128)}, f32[576,128]{1,0:T(8,128)S(1)}, u32[]{:S(2)}, u32[]{:S(2)}) collective-permute-start(f32[576,128]{1,0:T(8,128)} %get-tuple-element.34), channel_id=1, source_target_pairs={{0,96},{32,64},{64,32},{96,0},{1,97},{33,65},{65,33},{97,1},{2,98}... | collective-permute-start | bytes 884744 | tf_op jit(solution)/shard_map/ppermute | solution.py:491
  59.8 22.7 %pair_filters.1 = (bf16[57344,128]{1,0:T(8,128)(2,1)}, bf16[57344,128]{1,0:T(8,128)(2,1)}) custom-call(s32[8,128]{1,0:T(8,128)} %get-tuple-element.27.count, s32[1,1792]{1,0:T(1,128)} %get-tuple-element.28.order, f32[128,2048]{1,0:T(8,128)} %get-tuple-element.31.table, f32[1,128]{1,0:T(1,128)} %constant.34.clone.centres, bf16[128,128]{1,0:T(8,128)(2,1)} %first_128.1, ...), custom_call_target="tpu_custom_call" | custom-call | tf_op jit(solution)/shard_map/pair_filters/pallas_call | solution.py:317
  83.4 8.8 %messages_and_update.1 = (bf16[256,128]{1,0:T(8,128)(2,1)}, f32[256,128]{1,0:T(8,128)}) custom-call(s32[8,128]{1,0:T(8,128)} %get-tuple-element.27.count, s32[1,1792]{1,0:T(1,128)} %get-tuple-element.28.order, s32[1,1792]{1,0:T(1,128)} %get-tuple-element.29.own_rows, s32[1,1792]{1,0:T(1,128)} %get-tuple-element.30.other_rows, ...), custom_call_target="tpu_custom_call" | custom-call | tf_op jit(solution)/shard_map/messages_and_update/pallas_call | solution.py:471
  92.2 1.9 %collective-permute-start.6 = (f32[256,128]{1,0:T(8,128)}, f32[256,128]{1,0:T(8,128)S(1)}, u32[]{:S(2)}, u32[]{:S(2)}) collective-permute-start(f32[256,128]{1,0:T(8,128)} %get-tuple-element.37.own_g), channel_id=1, source_target_pairs={{0,1},{1,0},{2,3},{3,2},{4,5},{5,4},{6,7},{7,6},{8,9},{9,8},{10,11... | collective-permute-start | bytes 393224 | tf_op jit(solution)/shard_map/ppermute | solution.py:492
  94.1 1.9 %collective-permute-start.7 = (f32[256,128]{1,0:T(8,128)}, f32[256,128]{1,0:T(8,128)S(1)}, u32[]{:S(2)}, u32[]{:S(2)}) collective-permute-start(f32[256,128]{1,0:T(8,128)} %get-tuple-element.37.own_g), channel_id=1, source_target_pairs={{0,31},{1,2},{2,1},{3,4},{4,3},{5,6},{6,5},{7,8},{8,7},{9,10},{10,... | collective-permute-start | bytes 393224 | tf_op jit(solution)/shard_map/ppermute | solution.py:491
  96.1 0.9 constant_dynamic-update-slice_fusion.1
  97.0 9.6 %collective-permute-done.7 = f32[256,128]{1,0:T(8,128)S(1)} collective-permute-done((f32[256,128]{1,0:T(8,128)}, f32[256,128]{1,0:T(8,128)S(1)}, u32[]{:S(2)}, u32[]{:S(2)}) %collective-permute-start.7) | collective-permute-done | bytes 131104 | tf_op jit(solution)/shard_map/ppermute | solution.py:491
  106.6 1.9 %collective-permute-start.9 = (f32[768,128]{1,0:T(8,128)S(1)}, f32[768,128]{1,0:T(8,128)S(1)}, u32[]{:S(2)}, u32[]{:S(2)}) collective-permute-start(f32[768,128]{1,0:T(8,128)S(1)} %constant_dynamic-update-slice_fusion.middle.g1), channel_id=1, source_target_pairs={{0,384},{128,256},{256,128},{384,0},{1,385},{129,257},{257,129},{3... | collective-permute-start | bytes 1179656 | tf_op jit(solution)/shard_map/ppermute | solution.py:491
  108.6 4.8 %collective-permute-start.8 = (f32[768,128]{1,0:T(8,128)S(1)}, f32[768,128]{1,0:T(8,128)S(1)}, u32[]{:S(2)}, u32[]{:S(2)}) collective-permute-start(f32[768,128]{1,0:T(8,128)S(1)} %constant_dynamic-update-slice_fusion.middle.g1), channel_id=1, source_target_pairs={{0,128},{128,0},{256,384},{384,256},{1,129},{129,1},{257,385},{385... | collective-permute-start | bytes 1179656 | tf_op jit(solution)/shard_map/ppermute | solution.py:492
  113.4 4.1 %collective-permute-done.9.other_side.g2 = f32[768,128]{1,0:T(8,128)S(1)} collective-permute-done((f32[768,128]{1,0:T(8,128)S(1)}, f32[768,128]{1,0:T(8,128)S(1)}, u32[]{:S(2)}, u32[]{:S(2)}) %collective-permute-start.9) | collective-permute-done | bytes 393248 | tf_op jit(solution)/shard_map/ppermute | solution.py:491
  117.5 1.6 %collective-permute-done.8.one_side.g0 = f32[768,128]{1,0:T(8,128)S(1)} collective-permute-done((f32[768,128]{1,0:T(8,128)S(1)}, f32[768,128]{1,0:T(8,128)S(1)}, u32[]{:S(2)}, u32[]{:S(2)}) %collective-permute-start.8) | collective-permute-done | bytes 393248 | tf_op jit(solution)/shard_map/ppermute | solution.py:492
  119.2 0.8 copy-done.5
  119.9 3.0 %tiles_to_send.3 = (f32[576,128]{1,0:T(8,128)}, f32[576,128]{1,0:T(8,128)}) custom-call(s32[8,56]{1,0:T(8,128)} %get-tuple-element.23.lists, f32[768,128]{1,0:T(8,128)} %copy-done.5, f32[768,128]{1,0:T(8,128)} %copy-done.3, f32[768,128]{1,0:T(8,128)} %copy-done.4), custom_call_target="tpu_custom_call" | custom-call | tf_op jit(solution)/shard_map/tiles_to_send/pallas_call | solution.py:356
  123.0 2.4 %collective-permute-start.10 = (f32[576,128]{1,0:T(8,128)}, f32[576,128]{1,0:T(8,128)S(1)}, u32[]{:S(2)}, u32[]{:S(2)}) collective-permute-start(f32[576,128]{1,0:T(8,128)} %get-tuple-element.38), channel_id=1, source_target_pairs={{0,32},{32,0},{64,96},{96,64},{1,33},{33,1},{65,97},{97,65},{2,34}... | collective-permute-start | bytes 884744 | tf_op jit(solution)/shard_map/ppermute | solution.py:492
  125.3 6.8 %collective-permute-start.11 = (f32[576,128]{1,0:T(8,128)}, f32[576,128]{1,0:T(8,128)S(1)}, u32[]{:S(2)}, u32[]{:S(2)}) collective-permute-start(f32[576,128]{1,0:T(8,128)} %get-tuple-element.39), channel_id=1, source_target_pairs={{0,96},{32,64},{64,32},{96,0},{1,97},{33,65},{65,33},{97,1},{2,98}... | collective-permute-start | bytes 884744 | tf_op jit(solution)/shard_map/ppermute | solution.py:491
  132.8 1.0 copy.30
  133.8 1.1 pad.9.r_near
  134.9 5.3 %collective-permute-done.11.g4 = f32[576,128]{1,0:T(8,128)S(1)} collective-permute-done((f32[576,128]{1,0:T(8,128)}, f32[576,128]{1,0:T(8,128)S(1)}, u32[]{:S(2)}, u32[]{:S(2)}) %collective-permute-start.11) | collective-permute-done | bytes 294944 | tf_op jit(solution)/shard_map/ppermute | solution.py:491
  140.9 14.2 %pair_gradients.1 = (f32[256,128]{1,0:T(8,128)}, f32[3,256]{1,0:T(4,128)}) custom-call(s32[8,128]{1,0:T(8,128)} %get-tuple-element.27.count, s32[1,1792]{1,0:T(1,128)} %get-tuple-element.28.order, s32[1,1792]{1,0:T(1,128)} %get-tuple-element.29.own_rows, s32[1,1792]{1,0:T(1,128)} %get-tuple-element.30.other_rows, bf16[57344,128]{1,0:T(8,128)(2,1)} %get-tuple-element.32.filt, ...), custom_call_target="tpu_custom_call" | custom-call | tf_op jit(solution)/shard_map/pair_gradients/pallas_call | solution.py:471
  155.1 1.3 copy.31
  (50 shorter events, 7.3 us)
Async XLA Ops:
  0.6 131.5 %copy-start.12 = (f32[1,1,1,3,256]{4,2,3,1,0:T(1,128)S(1)}, f32[1,1,1,3,256]{4,2,3,1,0:T(1,128)}, u32[]{:S(2)}) copy-start(f32[1,1,1,3,256]{4,2,3,1,0:T(1,128)} %param.21) | copy-start | bytes 9220
  4.1 136.2 %copy-start.6 = (f32[256,128]{1,0:T(8,128)}, f32[256,128]{1,0:T(8,128)S(1)}, u32[]{:S(2)}) copy-start(f32[256,128]{1,0:T(8,128)S(1)} %fusion.own_h) | copy-start | bytes 393220
  4.2 17.8 %collective-permute-start.1 = (f32[1,264,128]{2,1,0:T(8,128)S(1)}, f32[1,264,128]{2,1,0:T(8,128)S(1)}, u32[]{:S(2)}, u32[]{:S(2)}) collective-permute-start(f32[1,264,128]{2,1,0:T(8,128)S(1)} %maximum_bitcast_fusion), channel_id=1, source_target_pairs={{0,31},{1,2},{2,1},{3,4},{4,3},{5,6},{6,5},{7,8},{8,7},{9,10},{10,... | collective-permute-start | bytes 405512 | tf_op jit(solution)/shard_map/ppermute | solution.py:491
  18.9 3.2 %collective-permute-start = (f32[1,264,128]{2,1,0:T(8,128)S(1)}, f32[1,264,128]{2,1,0:T(8,128)S(1)}, u32[]{:S(2)}, u32[]{:S(2)}) collective-permute-start(f32[1,264,128]{2,1,0:T(8,128)S(1)} %maximum_bitcast_fusion), channel_id=1, source_target_pairs={{0,1},{1,0},{2,3},{3,2},{4,5},{5,4},{6,7},{7,6},{8,9},{9,8},{10,11... | collective-permute-start | bytes 405512 | tf_op jit(solution)/shard_map/ppermute | solution.py:492
  22.2 28.7 %copy-start = (f32[3,256,128]{2,1,0:T(8,128)}, f32[3,256,128]{2,1,0:T(8,128)S(1)}, u32[]{:S(2)}) copy-start(f32[3,256,128]{2,1,0:T(8,128)S(1)} %pad_maximum_fusion) | copy-start | bytes 1179652
  22.2 28.7 %collective-permute-start.3 = (f32[768,128]{1,0:T(8,128)S(1)}, f32[768,128]{1,0:T(8,128)S(1)}, u32[]{:S(2)}, u32[]{:S(2)}) collective-permute-start(f32[768,128]{1,0:T(8,128)S(1)} %bitcast.35), channel_id=1, source_target_pairs={{0,384},{128,256},{256,128},{384,0},{1,385},{129,257},{257,129},{3... | collective-permute-start | bytes 1179656 | tf_op jit(solution)/shard_map/ppermute | solution.py:491
  26.9 24.0 %collective-permute-start.2 = (f32[768,128]{1,0:T(8,128)S(1)}, f32[768,128]{1,0:T(8,128)S(1)}, u32[]{:S(2)}, u32[]{:S(2)}) collective-permute-start(f32[768,128]{1,0:T(8,128)S(1)} %bitcast.36), channel_id=1, source_target_pairs={{0,128},{128,0},{256,384},{384,256},{1,129},{129,1},{257,385},{385... | collective-permute-start | bytes 1179656 | tf_op jit(solution)/shard_map/ppermute | solution.py:492
  29.7 13.5 %all-to-all-start = ((f32[16,24,128]{2,1,0:T(8,128)}), f32[16,24,128]{2,1,0:T(8,128)S(1)}, u32[]{:S(2)}, u32[]{:S(2)}) async-start(f32[16,24,128]{2,1,0:T(8,128)} %broadcast_in_dim.32), calls=%async_computation | async-start | bytes 393216 | tf_op jit(solution)/shard_map/all_to_all | solution.py:535
  50.9 81.8 %copy-start.11 = (f32[64,128]{1,0:T(8,128)S(1)}, f32[64,128]{1,0:T(8,128)}, u32[]{:S(2)}) copy-start(f32[64,128]{1,0:T(8,128)} %get-tuple-element.40) | copy-start | bytes 98308
  50.9 0.8 copy-start.1
  50.9 0.9 copy-start.2
  54.9 27.7 %collective-permute-start.4 = (f32[576,128]{1,0:T(8,128)}, f32[576,128]{1,0:T(8,128)S(1)}, u32[]{:S(2)}, u32[]{:S(2)}) collective-permute-start(f32[576,128]{1,0:T(8,128)} %get-tuple-element.33), channel_id=1, source_target_pairs={{0,32},{32,0},{64,96},{96,64},{1,33},{33,1},{65,97},{97,65},{2,34}... | collective-permute-start | bytes 884744 | tf_op jit(solution)/shard_map/ppermute | solution.py:492
  57.8 24.8 %collective-permute-start.5 = (f32[576,128]{1,0:T(8,128)}, f32[576,128]{1,0:T(8,128)S(1)}, u32[]{:S(2)}, u32[]{:S(2)}) collective-permute-start(f32[576,128]{1,0:T(8,128)} %get-tuple-element.34), channel_id=1, source_target_pairs={{0,96},{32,64},{64,32},{96,0},{1,97},{33,65},{65,33},{97,1},{2,98}... | collective-permute-start | bytes 884744 | tf_op jit(solution)/shard_map/ppermute | solution.py:491
  82.6 0.7 copy-start.7
  82.6 0.8 copy-start.8
  92.2 3.8 %collective-permute-start.6 = (f32[256,128]{1,0:T(8,128)}, f32[256,128]{1,0:T(8,128)S(1)}, u32[]{:S(2)}, u32[]{:S(2)}) collective-permute-start(f32[256,128]{1,0:T(8,128)} %get-tuple-element.37.own_g), channel_id=1, source_target_pairs={{0,1},{1,0},{2,3},{3,2},{4,5},{5,4},{6,7},{7,6},{8,9},{9,8},{10,11... | collective-permute-start | bytes 393224 | tf_op jit(solution)/shard_map/ppermute | solution.py:492
  94.1 12.5 %collective-permute-start.7 = (f32[256,128]{1,0:T(8,128)}, f32[256,128]{1,0:T(8,128)S(1)}, u32[]{:S(2)}, u32[]{:S(2)}) collective-permute-start(f32[256,128]{1,0:T(8,128)} %get-tuple-element.37.own_g), channel_id=1, source_target_pairs={{0,31},{1,2},{2,1},{3,4},{4,3},{5,6},{6,5},{7,8},{8,7},{9,10},{10,... | collective-permute-start | bytes 393224 | tf_op jit(solution)/shard_map/ppermute | solution.py:491
  106.6 12.5 %copy-start.3 = (f32[768,128]{1,0:T(8,128)}, f32[768,128]{1,0:T(8,128)S(1)}, u32[]{:S(2)}) copy-start(f32[768,128]{1,0:T(8,128)S(1)} %constant_dynamic-update-slice_fusion.middle.g1) | copy-start | bytes 1179652
  106.6 10.9 %collective-permute-start.9 = (f32[768,128]{1,0:T(8,128)S(1)}, f32[768,128]{1,0:T(8,128)S(1)}, u32[]{:S(2)}, u32[]{:S(2)}) collective-permute-start(f32[768,128]{1,0:T(8,128)S(1)} %constant_dynamic-update-slice_fusion.middle.g1), channel_id=1, source_target_pairs={{0,384},{128,256},{256,128},{384,0},{1,385},{129,257},{257,129},{3... | collective-permute-start | bytes 1179656 | tf_op jit(solution)/shard_map/ppermute | solution.py:491
  108.6 10.6 %collective-permute-start.8 = (f32[768,128]{1,0:T(8,128)S(1)}, f32[768,128]{1,0:T(8,128)S(1)}, u32[]{:S(2)}, u32[]{:S(2)}) collective-permute-start(f32[768,128]{1,0:T(8,128)S(1)} %constant_dynamic-update-slice_fusion.middle.g1), channel_id=1, source_target_pairs={{0,128},{128,0},{256,384},{384,256},{1,129},{129,1},{257,385},{385... | collective-permute-start | bytes 1179656 | tf_op jit(solution)/shard_map/ppermute | solution.py:492
  117.5 1.6 %copy-start.4 = (f32[768,128]{1,0:T(8,128)}, f32[768,128]{1,0:T(8,128)S(1)}, u32[]{:S(2)}) copy-start(f32[768,128]{1,0:T(8,128)S(1)} %collective-permute-done.9.other_side.g2) | copy-start | bytes 1179652
  119.2 0.8 copy-start.5
  123.0 12.0 %collective-permute-start.10 = (f32[576,128]{1,0:T(8,128)}, f32[576,128]{1,0:T(8,128)S(1)}, u32[]{:S(2)}, u32[]{:S(2)}) collective-permute-start(f32[576,128]{1,0:T(8,128)} %get-tuple-element.38), channel_id=1, source_target_pairs={{0,32},{32,0},{64,96},{96,64},{1,33},{33,1},{65,97},{97,65},{2,34}... | collective-permute-start | bytes 884744 | tf_op jit(solution)/shard_map/ppermute | solution.py:492
  125.3 14.9 %collective-permute-start.11 = (f32[576,128]{1,0:T(8,128)}, f32[576,128]{1,0:T(8,128)S(1)}, u32[]{:S(2)}, u32[]{:S(2)}) collective-permute-start(f32[576,128]{1,0:T(8,128)} %get-tuple-element.39), channel_id=1, source_target_pairs={{0,96},{32,64},{64,32},{96,0},{1,97},{33,65},{65,33},{97,1},{2,98}... | collective-permute-start | bytes 884744 | tf_op jit(solution)/shard_map/ppermute | solution.py:491
  134.9 5.3 %copy-start.9 = (f32[576,128]{1,0:T(8,128)}, f32[576,128]{1,0:T(8,128)S(1)}, u32[]{:S(2)}) copy-start(f32[576,128]{1,0:T(8,128)S(1)} %collective-permute-done.10.g3) | copy-start | bytes 884740
  140.2 0.7 copy-start.10
